TPU v7x, 256 devices: a whole 4x4x8 slice. The times are simulated.
256 devices in a mesh: dp: 8 (over z_lo, x), vocab: 32 (over y, z_hi, core).
Axes of the slice: x: 4, y: 4, z: 8 (z_hi: 4, z_lo: 2; z = z_hi * 2 + z_lo), core: 2. Of those that a mesh axis runs over, the one named last changes fastest.
Arguments:
- hidden_now: bfloat16 [1024, 3584], P('dp'), may hold values from -6 to 6
- hidden_next: bfloat16 [1024, 3584], P('dp'), may hold values from -100 to 100
- cotangent: bfloat16 [1024, 81920], P('dp', 'vocab'), may hold values from -6 to 6
- master: float32 [81920, 3584], P(('vocab', 'dp')), may hold values from -1 to 1
- moment: bfloat16 [81920, 3584], P(('vocab', 'dp')), may hold values from -19.2 to 19.2
- second: bfloat16 [81920, 3584], P(('vocab', 'dp')), may hold values from 2.048 to 20.48, as said below
- targets: int32 [1024], P('dp'), may hold values from 0 to 81919
Outputs:
- next_logits: bfloat16 [1024, 81920], P('dp', 'vocab')
- next_loss: float32 [1024], P('dp')
Inputs may be any that keep to these rules, and one draw needn't show every extreme that they name: `second`: Positive.
All inputs are finite; a program needn't handle non-finite values.
Results may differ from a plain program's by a relative error of at most 0.015.
Values may be sent and summed in bfloat16 or wider, within the bound.
No kernel may reach another device: no remote copies, remote signals or barrier semaphores. Data moves between devices by JAX's collectives and lax.ppermute only.
A program may use at most 128 MiB of HBM per device.

v0:
```python
import jax
import jax.numpy as jnp
from jax import lax
from jax.sharding import PartitionSpec as P

learn_rate = 0.02
beta_one = 0.9
beta_two = 0.95
epsilon = 1e-08
decay_rate = 0.1


def shards(hidden_now, hidden_next, cotangent, master, moment, second, targets):
    partial_grad = lax.dot_general(
        cotangent, hidden_now, (((0,), (0,)), ((), ())), preferred_element_type=jnp.float32
    )
    gradient = lax.psum_scatter(
        partial_grad.astype(jnp.bfloat16), "dp", scatter_dimension=0, tiled=True
    ).astype(jnp.float32)
    moment_new = beta_one * moment.astype(jnp.float32) + (1.0 - beta_one) * gradient
    second_new = beta_two * second.astype(jnp.float32) + (1.0 - beta_two) * gradient * gradient
    master_new = master - learn_rate * (
        moment_new / (jnp.sqrt(second_new) + epsilon) + decay_rate * master
    )
    head_rows = master_new.astype(jnp.bfloat16)
    owner_logits = lax.dot_general(
        lax.all_gather(hidden_next, "dp", axis=0, tiled=True),
        head_rows,
        (((1,), (1,)), ((), ())),
        preferred_element_type=jnp.float32,
    )
    logits = lax.all_to_all(
        owner_logits.astype(jnp.bfloat16), "dp", split_axis=0, concat_axis=1, tiled=True
    ).astype(owner_logits.dtype)
    offset = lax.axis_index("vocab") * logits.shape[1]
    local_target = targets - offset
    positions = lax.broadcasted_iota(jnp.int32, logits.shape, 1)
    picked = jnp.sum(jnp.where(positions == local_target[:, None], logits, 0.0), axis=1)
    row_top = lax.pmax(jnp.max(logits, axis=1), "vocab")
    local_total = jnp.sum(jnp.exp(logits - row_top[:, None]), axis=1)
    row_total, target_logit = lax.psum((local_total, picked), "vocab")
    row_loss = jnp.log(row_total) + row_top - target_logit
    next_rows = logits.astype(jnp.bfloat16)
    return (next_rows, row_loss)


def solution(mesh):
    in_specs = (
        P("dp", None),
        P("dp", None),
        P("dp", "vocab"),
        P(("vocab", "dp"), None),
        P(("vocab", "dp"), None),
        P(("vocab", "dp"), None),
        P("dp"),
    )
    out_specs = (P("dp", "vocab"), P("dp"))
    return jax.shard_map(shards, mesh=mesh, in_specs=in_specs, out_specs=out_specs, check_vma=False)
```

profile of v0, /device:TPU:1, one launch (start us, length us, event | category | flops | bytes accessed | tf_op | source)
XLA Modules:
  0.0 467.6 jit_solution(5824811596226031601)
XLA Ops:
  7.2 0.0 copy-start
  7.2 0.0 all-gather.2.cloned.1.call-start
  7.2 0.7 all-gather.2.cloned.1.call-update
  7.9 0.0 reduce-scatter.2.cloned.1.call-start
  8.0 0.4 copy-done
  8.3 10.0 %convolution_convert_fusion = bf16[2560,3584]{1,0:T(8,128)(2,1)} fusion(bf16[128,2560]{1,0:T(8,128)(2,1)} %param.9, bf16[128,3584]{1,0:T(8,128)(2,1)S(1)} %copy-done), kind=kOutput, calls=%fused_computation | convolution fusion | flops 2357985280 | bytes 19922944 | tf_op jit(solution)/shard_map/dot_general | solution.py:14
  18.3 0.0 copy-start.1
  18.3 0.0 reduce-scatter.2.cloned.1.call-update
  18.4 0.0 copy-start.2
  18.4 79.9 %all-gather.2.cloned.1.call-done = bf16[1024,3584]{1,0:T(8,128)(2,1)} async-done(((bf16[128,3584]{1,0:T(8,128)(2,1)}), bf16[1024,3584]{1,0:T(8,128)(2,1)}) %all-gather.2.cloned.1.call-update) | async-done | bytes 7340048 | tf_op jit(solution)/shard_map/all_gather | solution.py:27
  98.3 190.2 %reduce-scatter.2.cloned.1.call-done = bf16[320,3584]{1,0:T(8,128)(2,1)} async-done(((bf16[2560,3584]{1,0:T(8,128)(2,1)}), bf16[320,3584]{1,0:T(8,128)(2,1)}) %reduce-scatter.2.cloned.1.call-update) | async-done | bytes 2293776 | tf_op jit(solution)/shard_map/reduce_scatter | solution.py:17
  288.5 0.0 copy-done.1
  288.5 10.7 %fusion.17 = bf16[40,8,8,128]{3,2,1,0:T(8,128)(2,1)S(1)} fusion(bf16[1024,3584]{1,0:T(8,128)(2,1)} %all-gather.2.cloned.1.call-done, f32[320,3584]{1,0:T(8,128)} %param.10, bf16[320,3584]{1,0:T(8,128)(2,1)S(1)} %copy-done.1, bf16[320,3584]{1,0:T(8,128)(2,1)} %reduce-scatter.2.cloned.1.call-done, bf16[320,3584]{1,0:T(8,128)(2,1)} %param.11), kind=kOutput, calls=%fused_computation.19 | convolution fusion | flops 2368634880 | bytes 19464192 | tf_op jit(solution)/shard_map/dot_general | solution.py:26
  299.2 1.0 copy.14
  300.2 3.5 all-to-all-start
  303.7 0.0 copy-done.2
  303.8 9.9 %all-to-all-done = bf16[8,128,320]{1,2,0:T(8,128)(2,1)S(1)} async-done(((bf16[8,128,320]{1,2,0:T(8,128)(2,1)}), bf16[8,128,320]{1,2,0:T(8,128)(2,1)S(1)}, u32[]{:S(2)}, u32[]{:S(2)}) %all-to-all-start) | async-done | bytes 655392 | tf_op jit(solution)/shard_map/all_to_all | solution.py:32
  313.7 0.4 reduce_max.14
  314.1 70.8 %pmax.7 = f32[128]{0:T(128)S(1)} all-reduce(bf16[128]{0:T(256)(128)(2,1)S(1)} %reduce_max.14), channel_id=1, replica_groups=mesh['dp'=8,'vocab'=32] {'vocab'}, use_global_device_ids=true, to_apply=%region_2.3 | all-reduce | flops 128 | bytes 768 | tf_op jit(solution)/shard_map/pmax | solution.py:39
  384.8 1.1 copy.11
  385.9 0.5 fusion.15
  386.4 73.8 %all-reduce = (f32[128]{0:T(128)S(1)}, f32[128]{0:T(128)S(1)}) all-reduce(f32[128]{0:T(128)S(1)} %get-tuple-element.5, f32[128]{0:T(128)S(1)} %get-tuple-element.4), channel_id=1, replica_groups=mesh['dp'=8,'vocab'=32] {'vocab'}, use_global_device_ids=true, to_apply=%region_6.7 | all-reduce | flops 256 | bytes 2048 | tf_op jit(solution)/shard_map/psum | solution.py:41
  460.3 0.5 add_subtract_fusion
  (2 shorter events, 0.0 us)
Async XLA Ops:
  7.2 1.2 copy-start
  7.2 91.1 %all-gather.2.cloned.1.call-start = ((), (), s32[]{:S(2)}) async-start(), calls=%async_computation.3 | async-start | bytes 8257536 | tf_op jit(solution)/shard_map/all_gather | solution.py:27
  7.9 280.6 %reduce-scatter.2.cloned.1.call-start = ((), (), s32[]{:S(2)}) async-start(), calls=%async_computation.2 | async-start | bytes 20643840 | tf_op jit(solution)/shard_map/reduce_scatter | solution.py:17
  18.3 270.1 %copy-start.1 = (bf16[320,3584]{1,0:T(8,128)(2,1)S(1)}, bf16[320,3584]{1,0:T(8,128)(2,1)}, u32[]{:S(2)}) copy-start(bf16[320,3584]{1,0:T(8,128)(2,1)} %param.12) | copy-start | bytes 6881284
  18.4 285.4 %copy-start.2 = (s32[128]{0:T(128)S(1)}, s32[128]{0:T(128)}, u32[]{:S(2)}) copy-start(s32[128]{0:T(128)} %param.13) | copy-start | bytes 1540
  300.2 13.5 %all-to-all-start = ((bf16[8,128,320]{1,2,0:T(8,128)(2,1)}), bf16[8,128,320]{1,2,0:T(8,128)(2,1)S(1)}, u32[]{:S(2)}, u32[]{:S(2)}) async-start(bf16[8,128,320]{1,2,0:T(8,128)(2,1)} %bitcast.13), calls=%async_computation.1 | async-start | bytes 1310720 | tf_op jit(solution)/shard_map/all_to_all | solution.py:32
Sparse Core Ops, SparseCore 0:
  9.8 88.4 all-gather.1
  100.9 187.4 reduce-scatter.1
where the time goes:
time: 468 us
  waiting for transfers between devices  281 us (60%)
  blocking collectives  145 us (31%)
  matrix products  20.7 us (4%)
  between operations  14.1 us (3%)
    reduce_scatter x1, waiting for transfers between devices, shards(): lax.psum_scatter(partial_grad.astype(jnp.bfloat16), 'dp', scatter_dimensi...  190 us
    all_gather x1, waiting for transfers between devices, shards(): lax.all_gather(hidden_next, 'dp', axis=0, tiled=True)  79.9 us
    psum x1, blocking collectives, shards(): row_total, target_logit = lax.psum((local_total, picked), 'vocab')  73.8 us
    pmax x1, blocking collectives, shards(): row_top = lax.pmax(jnp.max(logits, axis=1), 'vocab')  70.8 us
    dot_general x1, matrix products, shards(): lax.dot_general(lax.all_gather(hidden_next, 'dp', axis=0, tiled=True), he...  10.7 us
    dot_general x1, matrix products, shards(): lax.dot_general(cotangent, hidden_now, (((0,), (0,)), ((), ())), preferre...  9.99 us
    all_to_all x1, waiting for transfers between devices, shards(): lax.all_to_all(owner_logits.astype(jnp.bfloat16), 'dp', split_axis=0, con...  9.95 us
  transfers between devices with their start and end apart: 3, of which 3 were waited for; matrix products, arithmetic and copies ran while one was open for 2% of the time, Pallas kernels for 0%

commit v1 on v0

v1 whole, which is shorter than its diff:
```python
import jax
import jax.numpy as jnp
from jax import lax
from jax.experimental import pallas as pl
from jax.experimental.pallas import tpu as pltpu
from jax.sharding import PartitionSpec as P

learn_rate = 0.02
beta_one = 0.9
beta_two = 0.95
epsilon = 1e-08
decay_rate = 0.1

NX, NZL, NY, NZH, NC = 4, 2, 4, 4, 2
N_DP, N_VOCAB = NX * NZL, NY * NZH * NC
TOK = 128
HALF = TOK // 2
Q = HALF // 2
ROWS = 320
BLOCK = 512
BF16 = jnp.bfloat16
F32 = jnp.float32


def device_number(zl, x, y, zh, core):
    return (zl * NX + x) * N_VOCAB + (y * NZH + zh) * NC + core


def shift_pairs(dx, dz, flip):
    pairs = []
    for zl in range(NZL):
        for x in range(NX):
            for y in range(NY):
                for zh in range(NZH):
                    for core in range(NC):
                        z = (zh * 2 + zl + dz) % 8
                        source = device_number(z % 2, (x + dx) % NX, y, z // 2, core ^ flip)
                        pairs.append((source, device_number(zl, x, y, zh, core)))
    return pairs


def receive(value, dx=0, dz=0, flip=0):
    return lax.ppermute(value, ("dp", "vocab"), shift_pairs(dx, dz, flip))


A, B = 0, 1
LAYOUT = (
    (0, 1, A, 0, HALF), (HALF, 1, B, 0, HALF),
    (2 * HALF, 3, A, 0, HALF), (3 * HALF, 3, B, 0, HALF),
    (4 * HALF, 4, A, 0, HALF), (5 * HALF, 4, B, 0, HALF),
    (6 * HALF, 2, A, 0, HALF), (7 * HALF, 5, A, 0, Q),
    (7 * HALF + Q, 2, B, 0, HALF), (8 * HALF + Q, 7, B, Q, Q),
    (9 * HALF, 5, A, Q, Q), (9 * HALF + Q, 5, B, 0, HALF),
    (10 * HALF + Q, 7, A, 0, HALF), (11 * HALF + Q, 7, B, 0, Q),
    (12 * HALF, 6, A, 0, Q), (12 * HALF + Q, 6, B, Q, Q),
    (13 * HALF, 6, A, Q, Q), (13 * HALF + Q, 6, B, 0, Q),
)


def gather(hidden_now, hidden_next, core):
    start = core * HALF
    own = jnp.concatenate(
        [lax.dynamic_slice_in_dim(v, start, HALF, 0) for v in (hidden_now, hidden_next)], axis=0
    )
    a1, a2 = receive(own, dx=1), receive(own, dx=-1)
    b1, b2 = receive(own[:HALF], dz=1), receive(own[HALF:], dz=-1)
    r1 = receive(jnp.concatenate([a1, a2, b1, b2], axis=0), flip=1)
    c1 = receive(jnp.concatenate([a1[:HALF], b1[:Q]], axis=0), dx=1)
    c2 = receive(jnp.concatenate([a2[HALF:], b2[Q:]], axis=0), dx=-1)
    d1, d2 = receive(a1[Q:], dz=1), receive(a2[: 3 * Q], dz=-1)
    r2 = receive(jnp.concatenate([c1, c2, d1, d2], axis=0), flip=1)
    e1, e2 = receive(c1[HALF:], dx=1), receive(c2[HALF:], dx=-1)
    e3, e4 = receive(c1[Q:HALF], dz=1), receive(c2[:Q], dz=-1)
    r3 = receive(jnp.concatenate([e1, e2, e3, e4], axis=0), flip=1)
    return [a1, a2, b1, b2, c1, c2, d1, d2, e1, e2, e3, e4], [r1, r2, r3]


def plan(pieces):
    bounds = []
    at = 0
    for number, piece in enumerate(pieces):
        bounds.append((at, at + piece.shape[0], number))
        at += piece.shape[0]
    out = []
    for first, rank, array, row, rows in LAYOUT:
        (begin, number), = [(b, n) for b, e, n in bounds if b <= first and first + rows <= e]
        out.append((number, first - begin, rank, array, row, rows))
    return out


def update_kernel(mine, other, n_mine, place, now_ref, next_ref, *refs):
    n = n_mine + 3
    pieces, (cot_ref, master_ref, moment_ref, second_ref, out_ref, cot_t, blocks, total) = refs[:n], refs[n:]
    step = pl.program_id(0)

    @pl.when(step == 0)
    def _():
        for g in range(N_DP):
            cot_t[:, g * TOK : (g + 1) * TOK] = cot_ref[g]
        total[...] = jnp.zeros_like(total)

    for array, ref in ((A, now_ref), (B, next_ref)):
        blocks[array, pl.ds(pl.multiple_of(place[0], TOK), TOK), :] = ref[...]
    for table, first_ref, core_at in ((mine, 0, 8), (other, n_mine, 9)):
        for number, first, rank, array, row, rows in table:
            at = pl.multiple_of(place[rank] + place[core_at] + row, Q)
            blocks[array, pl.ds(at, rows), :] = pieces[first_ref + number][first : first + rows, :]

    gradient = jnp.dot(cot_t[...], blocks[A], preferred_element_type=F32)
    moment_new = beta_one * moment_ref[...].astype(F32) + (1.0 - beta_one) * gradient
    second_new = beta_two * second_ref[...].astype(F32) + (1.0 - beta_two) * gradient * gradient
    master = master_ref[...]
    rows_new = master - learn_rate * (moment_new / (jnp.sqrt(second_new) + epsilon) + decay_rate * master)
    total[...] += lax.dot_general(
        rows_new.astype(BF16), blocks[B], (((1,), (1,)), ((), ())), preferred_element_type=F32
    )

    @pl.when(step == pl.num_programs(0) - 1)
    def _():
        for g in range(N_DP):
            out_ref[g] = total[:, g * TOK : (g + 1) * TOK].astype(BF16)


def update_and_logits(place, hidden_now, hidden_next, mine, other, cot, master, moment, second):
    width = master.shape[1]
    column = lambda rows: pl.BlockSpec((rows, BLOCK), lambda j, place: (0, j))
    whole = pl.BlockSpec((N_DP, ROWS, TOK), lambda j, place: (0, 0, 0))
    pieces = list(mine) + list(other)
    kernel = lambda *refs: update_kernel(plan(mine), plan(other), len(mine), *refs)
    return pl.pallas_call(
        kernel,
        out_shape=jax.ShapeDtypeStruct((N_DP, ROWS, TOK), BF16),
        grid_spec=pltpu.PrefetchScalarGridSpec(
            num_scalar_prefetch=1,
            grid=(width // BLOCK,),
            in_specs=[column(TOK), column(TOK)]
            + [column(p.shape[0]) for p in pieces]
            + [whole, column(ROWS), column(ROWS), column(ROWS)],
            out_specs=whole,
            scratch_shapes=[
                pltpu.VMEM((ROWS, N_DP * TOK), BF16),
                pltpu.VMEM((2, N_DP * TOK, BLOCK), BF16),
                pltpu.VMEM((ROWS, N_DP * TOK), F32),
            ],
        ),
        compiler_params=pltpu.CompilerParams(vmem_limit_bytes=32 * 2**20),
        cost_estimate=pl.CostEstimate(flops=9_400_000_000, bytes_accessed=24_000_000, transcendentals=2_300_000),
        name="update_and_logits",
    )(place, hidden_now, hidden_next, *pieces, cot, master, moment, second)


def stats_kernel(logits_ref, target_ref, out_ref, stat_ref):
    value = logits_ref[...]
    wide = value.astype(F32)
    top = jnp.max(wide, axis=0, keepdims=True)
    sums = jnp.sum(jnp.exp(wide - top), axis=0, keepdims=True)
    positions = lax.broadcasted_iota(jnp.int32, wide.shape, 0)
    picked = jnp.sum(jnp.where(positions == target_ref[...], wide, 0.0), axis=0, keepdims=True)
    stats = jnp.concatenate([top, sums, picked], axis=0)
    stat_ref[...] = jnp.broadcast_to(stats[None], stat_ref.shape)
    out_ref[...] = value.T


def stats(logits_t, local_target):
    return pl.pallas_call(
        stats_kernel,
        out_shape=(
            jax.ShapeDtypeStruct((TOK, N_DP * ROWS), BF16),
            jax.ShapeDtypeStruct((N_VOCAB, 3, TOK), F32),
        ),
        name="stats",
    )(logits_t, local_target)


def loss_kernel(stat_ref, out_ref):
    value = stat_ref[...]
    top, sums, picked = value[:, 0], value[:, 1], value[:, 2]
    row_top = jnp.max(top, axis=0, keepdims=True)
    row_total = jnp.sum(sums * jnp.exp(top - row_top), axis=0, keepdims=True)
    out_ref[...] = jnp.log(row_total) + row_top - jnp.sum(picked, axis=0, keepdims=True)


def loss(stat):
    out = pl.pallas_call(
        loss_kernel, out_shape=jax.ShapeDtypeStruct((1, TOK), F32), name="loss"
    )(stat)
    return out.reshape(TOK)


def shards(hidden_now, hidden_next, cotangent, master, moment, second, targets):
    dp, vocab = lax.axis_index("dp"), lax.axis_index("vocab")
    core = vocab % NC
    ranks = [(((dp // NX + r // NX) % NZL) * NX + (dp + r % NX) % NX) * TOK for r in range(N_DP)]
    place = jnp.stack([r.astype(jnp.int32) for r in ranks + [core * HALF, (1 - core) * HALF]])
    cot = lax.all_to_all(cotangent.T.reshape(N_DP, ROWS, TOK), "dp", 0, 0)
    mine, other = gather(hidden_now, hidden_next, core)
    logits = update_and_logits(place, hidden_now, hidden_next, mine, other, cot, master, moment, second)
    logits = lax.all_to_all(logits, "dp", 0, 0).reshape(N_DP * ROWS, TOK)
    local_target = (targets - vocab * (N_DP * ROWS)).reshape(1, TOK)
    next_logits, stat = stats(logits, local_target)
    return next_logits, loss(lax.all_to_all(stat, "vocab", 0, 0))


def solution(mesh):
    in_specs = (
        P("dp", None),
        P("dp", None),
        P("dp", "vocab"),
        P(("vocab", "dp"), None),
        P(("vocab", "dp"), None),
        P(("vocab", "dp"), None),
        P("dp"),
    )
    out_specs = (P("dp", "vocab"), P("dp"))
    return jax.shard_map(shards, mesh=mesh, in_specs=in_specs, out_specs=out_specs, check_vma=False)
```

time: 468 us -> 147 us (0.31)
  waiting for transfers between devices: 281 us -> 47.9 us
  blocking collectives: 145 us -> 20.1 us
  starting transfers between devices: 3.62 us -> 35.5 us
  matrix products: 20.7 us -> 0 us
  Pallas kernels: 0 us -> 17.8 us
  local copies, waits for them, and re-layouts: 2.45 us -> 17.7 us
  between operations: 14.1 us -> 0.81 us
  other arithmetic: 1.41 us -> 6.36 us
    reduce_scatter x1 -> x0, waiting for transfers between devices: 190 us -> none  [shards(): lax.psum_scatter(partial_grad.astype(jnp.bfloat16), 'dp', scatter_dimensi...]
    all_gather x1 -> x0, waiting for transfers between devices: 79.9 us -> none  [shards(): lax.all_gather(hidden_next, 'dp', axis=0, tiled=True)]
    psum x1 -> x0, blocking collectives: 73.8 us -> none  [shards(): row_total, target_logit = lax.psum((local_total, picked), 'vocab')]
    pmax x1 -> x0, blocking collectives: 70.8 us -> none  [shards(): row_top = lax.pmax(jnp.max(logits, axis=1), 'vocab')]
    ppermute x0 -> x15, waiting for transfers between devices: none -> 34.3 us  [receive(): return lax.ppermute(value, ('dp', 'vocab'), shift_pairs(dx, dz, flip))]
    ppermute x0 -> x15, starting transfers between devices: none -> 25.8 us  [receive(): return lax.ppermute(value, ('dp', 'vocab'), shift_pairs(dx, dz, flip))]
    dot_general x2 -> x0, matrix products: 20.7 us -> none  [the longest x1 10.7 us: shards(): lax.dot_general(lax.all_gather(hidden_next, 'dp', axis=0, tiled=True), he...]
    all_to_all x0 -> x1, blocking collectives: none -> 20.1 us  [shards(): return (next_logits, loss(lax.all_to_all(stat, 'vocab', 0, 0)))]
  transfers between devices with their start and end apart: 3 -> 17, of which waited for: 3 -> 11; matrix products, arithmetic and copies ran while one was open for 2% -> 7% of each run, Pallas kernels for 0% -> 0%
where the time goes in v1:
time: 147 us; the launch traced here: 146 us
  waiting for transfers between devices  47.9 us (33%)
  starting transfers between devices  35.5 us (24%)
  blocking collectives  20.1 us (14%)
  Pallas kernels  17.8 us (12%)
  local copies, waits for them, and re-layouts  17.7 us (12%)
  other arithmetic  6.36 us (4%)
    ppermute x15, waiting for transfers between devices, receive(): return lax.ppermute(value, ('dp', 'vocab'), shift_pairs(dx, dz, flip))  34.3 us
    ppermute x15, starting transfers between devices, receive(): return lax.ppermute(value, ('dp', 'vocab'), shift_pairs(dx, dz, flip))  25.8 us
    all_to_all x1, blocking collectives, shards(): return (next_logits, loss(lax.all_to_all(stat, 'vocab', 0, 0)))  20.1 us
    pallas_call x1, Pallas kernels, update_and_logits(): pl.pallas_call(kernel, out_shape=jax.ShapeDtypeStruct((N_DP, ROWS, TOK),...  13.8 us
    unnamed x30, local copies, waits for them, and re-layouts  11.6 us
    all_to_all x1, waiting for transfers between devices, shards(): logits = lax.all_to_all(logits, 'dp', 0, 0).reshape(N_DP * ROWS, TOK)  9.03 us
    all_to_all x1, starting transfers between devices, shards(): logits = lax.all_to_all(logits, 'dp', 0, 0).reshape(N_DP * ROWS, TOK)  4.95 us
    all_to_all x1, starting transfers between devices, shards(): cot = lax.all_to_all(cotangent.T.reshape(N_DP, ROWS, TOK), 'dp', 0, 0)  4.69 us
  transfers between devices with their start and end apart: 17, of which 11 were waited for; matrix products, arithmetic and copies ran while one was open for 7% of the time, Pallas kernels for 0%

profile of v1, /device:TPU:1, one launch (start us, length us, event | category | flops | bytes accessed | tf_op | source)
XLA Modules:
  0.0 146.1 jit_solution(4755178081407948268)
XLA Ops:
  2.8 3.4 %collective-permute-start = (bf16[128,3584]{1,0:T(8,128)(2,1)S(1)}, bf16[128,3584]{1,0:T(8,128)(2,1)S(1)}, u32[]{:S(2)}, u32[]{:S(2)}) collective-permute-start(bf16[128,3584]{1,0:T(8,128)(2,1)S(1)} %pad_maximum_fusion.2), channel_id=1, source_target_pairs={{32,0},{33,1},{34,2},{35,3},{36,4},{37,5},{38,6},{39,7},{40,8},{41... | collective-permute-start | bytes 2752520 | tf_op jit(solution)/shard_map/ppermute | solution.py:43
  6.2 5.6 %collective-permute-start.2 = (bf16[64,3584]{1,0:T(8,128)(2,1)S(1)}, bf16[64,3584]{1,0:T(8,128)(2,1)S(1)}, u32[]{:S(2)}, u32[]{:S(2)}) collective-permute-start(bf16[64,3584]{1,0:T(8,128)(2,1)S(1)} %constant_dynamic-slice_fusion.1), channel_id=1, source_target_pairs={{128,0},{129,1},{130,2},{131,3},{132,4},{133,5},{134,6},{135,7},{1... | collective-permute-start | bytes 1376264 | tf_op jit(solution)/shard_map/ppermute | solution.py:43
  11.8 8.9 %collective-permute-done.2.refs_5_ = bf16[64,3584]{1,0:T(8,128)(2,1)S(1)} collective-permute-done((bf16[64,3584]{1,0:T(8,128)(2,1)S(1)}, bf16[64,3584]{1,0:T(8,128)(2,1)S(1)}, u32[]{:S(2)}, u32[]{:S(2)}) %collective-permute-start.2) | collective-permute-done | bytes 458784 | tf_op jit(solution)/shard_map/ppermute | solution.py:43
  20.7 3.1 %collective-permute-done.3.refs_6_ = bf16[64,3584]{1,0:T(8,128)(2,1)S(1)} collective-permute-done((bf16[64,3584]{1,0:T(8,128)(2,1)S(1)}, bf16[64,3584]{1,0:T(8,128)(2,1)S(1)}, u32[]{:S(2)}, u32[]{:S(2)}) %collective-permute-start.3) | collective-permute-done | bytes 458784 | tf_op jit(solution)/shard_map/ppermute | solution.py:43
  23.8 1.4 collective-permute-done.refs_3_
  25.3 3.5 %collective-permute-start.4 = (bf16[96,3584]{1,0:T(8,128)(2,1)S(1)}, bf16[96,3584]{1,0:T(8,128)(2,1)S(1)}, u32[]{:S(2)}, u32[]{:S(2)}) collective-permute-start(bf16[96,3584]{1,0:T(8,128)(2,1)S(1)} %pad_maximum_fusion.4), channel_id=1, source_target_pairs={{32,0},{33,1},{34,2},{35,3},{36,4},{37,5},{38,6},{39,7},{40,8},{41... | collective-permute-start | bytes 2064392 | tf_op jit(solution)/shard_map/ppermute | solution.py:43
  28.8 4.8 %collective-permute-done.1.refs_4_ = bf16[128,3584]{1,0:T(8,128)(2,1)S(1)} collective-permute-done((bf16[128,3584]{1,0:T(8,128)(2,1)S(1)}, bf16[128,3584]{1,0:T(8,128)(2,1)S(1)}, u32[]{:S(2)}, u32[]{:S(2)}) %collective-permute-start.1) | collective-permute-done | bytes 917536 | tf_op jit(solution)/shard_map/ppermute | solution.py:43
  33.8 2.5 %collective-permute-start.6 = (bf16[96,3584]{1,0:T(8,128)(2,1)S(1)}, bf16[96,3584]{1,0:T(8,128)(2,1)S(1)}, u32[]{:S(2)}, u32[]{:S(2)}) collective-permute-start(bf16[96,3584]{1,0:T(8,128)(2,1)S(1)} %slice.44), channel_id=1, source_target_pairs={{128,0},{129,1},{130,2},{131,3},{132,4},{133,5},{134,6},{135,7},{1... | collective-permute-start | bytes 2064392 | tf_op jit(solution)/shard_map/ppermute | solution.py:43
  36.5 1.7 %pad_maximum_fusion = bf16[384,3584]{1,0:T(8,128)(2,1)} fusion(bf16[64,3584]{1,0:T(8,128)(2,1)S(1)} %collective-permute-done.3.refs_6_, bf16[64,3584]{1,0:T(8,128)(2,1)S(1)} %collective-permute-done.2.refs_5_, bf16[128,3584]{1,0:T(8,128)(2,1)S(1)} %collective-permute-done.1.refs_4_, bf16[128,3584]{1,0:T(8,128)(2,1)S(1)} %collective-permute-done.refs_3_), kind=kLoop, calls=%fused_computation | loop fusion | flops 11010048 | bytes 5505024 | tf_op jit(solution)/shard_map/concatenate | solution.py:67
  38.2 2.7 %collective-permute-start.12 = (bf16[384,3584]{1,0:T(8,128)(2,1)}, bf16[384,3584]{1,0:T(8,128)(2,1)}, u32[]{:S(2)}, u32[]{:S(2)}) collective-permute-start(bf16[384,3584]{1,0:T(8,128)(2,1)} %pad_maximum_fusion), channel_id=1, source_target_pairs={{1,0},{0,1},{3,2},{2,3},{5,4},{4,5},{7,6},{6,7},{9,8},{8,9},{11,10... | collective-permute-start | bytes 8257544 | tf_op jit(solution)/shard_map/ppermute | solution.py:43
  42.0 7.8 %collective-permute-done.5.refs_8_ = bf16[96,3584]{1,0:T(8,128)(2,1)S(1)} collective-permute-done((bf16[96,3584]{1,0:T(8,128)(2,1)S(1)}, bf16[96,3584]{1,0:T(8,128)(2,1)S(1)}, u32[]{:S(2)}, u32[]{:S(2)}) %collective-permute-start.5) | collective-permute-done | bytes 688160 | tf_op jit(solution)/shard_map/ppermute | solution.py:43
  49.8 2.1 %collective-permute-done.7.refs_10_ = bf16[96,3584]{1,0:T(8,128)(2,1)S(1)} collective-permute-done((bf16[96,3584]{1,0:T(8,128)(2,1)S(1)}, bf16[96,3584]{1,0:T(8,128)(2,1)S(1)}, u32[]{:S(2)}, u32[]{:S(2)}) %collective-permute-start.7) | collective-permute-done | bytes 688160 | tf_op jit(solution)/shard_map/ppermute | solution.py:43
  51.9 1.8 %pad_maximum_fusion.1 = bf16[384,3584]{1,0:T(8,128)(2,1)} fusion(bf16[96,3584]{1,0:T(8,128)(2,1)S(1)} %collective-permute-done.7.refs_10_, bf16[96,3584]{1,0:T(8,128)(2,1)S(1)} %collective-permute-done.6.refs_9_, bf16[96,3584]{1,0:T(8,128)(2,1)S(1)} %collective-permute-done.5.refs_8_, bf16[96,3584]{1,0:T(8,128)(2,1)S(1)} %collective-permute-done.4.refs_7_), kind=kLoop, calls=%fused_computation.1 | loop fusion | flops 11010048 | bytes 5505024 | tf_op jit(solution)/shard_map/concatenate | solution.py:71
  53.7 3.6 %collective-permute-start.13 = (bf16[384,3584]{1,0:T(8,128)(2,1)}, bf16[384,3584]{1,0:T(8,128)(2,1)}, u32[]{:S(2)}, u32[]{:S(2)}) collective-permute-start(bf16[384,3584]{1,0:T(8,128)(2,1)} %pad_maximum_fusion.1), channel_id=1, source_target_pairs={{1,0},{0,1},{3,2},{2,3},{5,4},{4,5},{7,6},{6,7},{9,8},{8,9},{11,10... | collective-permute-start | bytes 8257544 | tf_op jit(solution)/shard_map/ppermute | solution.py:43
  58.0 2.7 %collective-permute-start.8 = (bf16[32,3584]{1,0:T(8,128)(2,1)S(1)}, bf16[32,3584]{1,0:T(8,128)(2,1)S(1)}, u32[]{:S(2)}, u32[]{:S(2)}) collective-permute-start(bf16[32,3584]{1,0:T(8,128)(2,1)S(1)} %get-tuple-element.9), channel_id=1, source_target_pairs={{32,0},{33,1},{34,2},{35,3},{36,4},{37,5},{38,6},{39,7},{40,8},{41... | collective-permute-start | bytes 688136 | tf_op jit(solution)/shard_map/ppermute | solution.py:43
  61.6 4.2 %collective-permute-done.8.refs_11_ = bf16[32,3584]{1,0:T(8,128)(2,1)S(1)} collective-permute-done((bf16[32,3584]{1,0:T(8,128)(2,1)S(1)}, bf16[32,3584]{1,0:T(8,128)(2,1)S(1)}, u32[]{:S(2)}, u32[]{:S(2)}) %collective-permute-start.8) | collective-permute-done | bytes 229408 | tf_op jit(solution)/shard_map/ppermute | solution.py:43
  65.7 2.2 %copy.9 = bf16[2560,128]{1,0:T(8,128)(2,1)} copy(bf16[2560,128]{0,1:T(8,128)(2,1)} %bitcast.18) | data formatting | bytes 1310720 | tf_op jit(solution)/shard_map/transpose | solution.py:195
  67.9 4.7 %all-to-all-start = ((bf16[8,320,128]{2,1,0:T(8,128)(2,1)}), bf16[8,320,128]{2,1,0:T(8,128)(2,1)}, u32[]{:S(2)}, u32[]{:S(2)}) async-start(bf16[8,320,128]{2,1,0:T(8,128)(2,1)} %bitcast.16), calls=%async_computation | async-start | bytes 1310720 | tf_op jit(solution)/shard_map/all_to_all | solution.py:195
  73.6 2.2 %pad_maximum_fusion.3 = bf16[128,3584]{1,0:T(8,128)(2,1)} fusion(bf16[32,3584]{1,0:T(8,128)(2,1)} %collective-permute-done.11.refs_14_, bf16[32,3584]{1,0:T(8,128)(2,1)} %collective-permute-done.10.refs_13_, bf16[32,3584]{1,0:T(8,128)(2,1)} %collective-permute-done.9.refs_12_, bf16[32,3584]{1,0:T(8,128)(2,1)S(1)} %collective-permute-done.8.refs_11_), kind=kLoop, calls=%fused_computation.3 | loop fusion | flops 3670016 | bytes 1835008 | tf_op jit(solution)/shard_map/concatenate | solution.py:74
  75.8 1.7 %collective-permute-start.14 = (bf16[128,3584]{1,0:T(8,128)(2,1)}, bf16[128,3584]{1,0:T(8,128)(2,1)}, u32[]{:S(2)}, u32[]{:S(2)}) collective-permute-start(bf16[128,3584]{1,0:T(8,128)(2,1)} %pad_maximum_fusion.3), channel_id=1, source_target_pairs={{1,0},{0,1},{3,2},{2,3},{5,4},{4,5},{7,6},{6,7},{9,8},{8,9},{11,10... | collective-permute-start | bytes 2752520 | tf_op jit(solution)/shard_map/ppermute | solution.py:43
  77.6 4.6 %all-to-all-done.refs_18_ = bf16[8,320,128]{2,1,0:T(8,128)(2,1)} async-done(((bf16[8,320,128]{2,1,0:T(8,128)(2,1)}), bf16[8,320,128]{2,1,0:T(8,128)(2,1)}, u32[]{:S(2)}, u32[]{:S(2)}) %all-to-all-start) | async-done | bytes 655392 | tf_op jit(solution)/shard_map/all_to_all | solution.py:195
  84.2 1.1 copy-done.5
  86.4 1.2 copy-done.9
  87.6 1.2 copy-done.10
  88.8 1.6 %copy-done.11 = bf16[320,3584]{1,0:T(8,128)(2,1)S(1)} copy-done((bf16[320,3584]{1,0:T(8,128)(2,1)S(1)}, bf16[320,3584]{1,0:T(8,128)(2,1)}, u32[]{:S(2)}) %copy-start.11) | copy-done | bytes 2293784
  90.4 1.6 %copy-done.12 = bf16[320,3584]{1,0:T(8,128)(2,1)S(1)} copy-done((bf16[320,3584]{1,0:T(8,128)(2,1)S(1)}, bf16[320,3584]{1,0:T(8,128)(2,1)}, u32[]{:S(2)}) %copy-start.12) | copy-done | bytes 2293784
  92.1 13.8 %update_and_logits.1 = bf16[8,320,128]{2,1,0:T(8,128)(2,1)S(1)} custom-call(s32[10]{0:T(128)S(1)} %stack.43.refs_0_, bf16[128,3584]{1,0:T(8,128)(2,1)S(1)} %copy-done.9, bf16[128,3584]{1,0:T(8,128)(2,1)S(1)} %copy-done.10, bf16[128,3584]{1,0:T(8,128)(2,1)S(1)} %collective-permute-done.refs_3_, bf16[128,3584]{1,0:T(8,128)(2,1)S(1)} %collective-permute-done.1.refs_4_, ...), custom_call_target="tpu_custom_call" | custom-call | flops 9400000512 | bytes 24000000 | tf_op jit(solution)/shard_map/update_and_logits/pallas_call | solution.py:130
  106.7 4.9 %all-to-all-start.1 = ((bf16[8,320,128]{2,1,0:T(8,128)(2,1)}), bf16[8,320,128]{2,1,0:T(8,128)(2,1)S(1)}, u32[]{:S(2)}, u32[]{:S(2)}) async-start(bf16[8,320,128]{2,1,0:T(8,128)(2,1)} %copy-done.8), calls=%async_computation.1 | async-start | bytes 1310720 | tf_op jit(solution)/shard_map/all_to_all | solution.py:198
  112.2 9.0 %all-to-all-done.1 = bf16[8,320,128]{2,1,0:T(8,128)(2,1)S(1)} async-done(((bf16[8,320,128]{2,1,0:T(8,128)(2,1)}), bf16[8,320,128]{2,1,0:T(8,128)(2,1)S(1)}, u32[]{:S(2)}, u32[]{:S(2)}) %all-to-all-start.1) | async-done | bytes 655392 | tf_op jit(solution)/shard_map/all_to_all | solution.py:198
  122.0 2.6 %stats.1 = (bf16[128,2560]{1,0:T(8,128)(2,1)}, f32[32,3,128]{2,1,0:T(4,128)}) custom-call(bf16[2560,128]{1,0:T(8,128)(2,1)} %bitcast.17, s32[1,128]{1,0:T(1,128)} %subtract_bitcast_fusion.target_ref), custom_call_target="tpu_custom_call" | custom-call | tf_op jit(solution)/shard_map/stats/pallas_call | solution.py:165
  124.7 20.1 %all_to_all.15.stat_ref = f32[32,3,128]{2,1,0:T(4,128)} all-to-all(f32[32,3,128]{2,1,0:T(4,128)} %get-tuple-element.5), channel_id=1, replica_groups=mesh['dp'=8,'vocab'=32] {'vocab'}, dimensions={0} | all-to-all | bytes 98304 | tf_op jit(solution)/shard_map/all_to_all | solution.py:201
  144.7 1.4 loss.1
  (55 shorter events, 11.8 us)
Async XLA Ops:
  2.8 22.4 %collective-permute-start = (bf16[128,3584]{1,0:T(8,128)(2,1)S(1)}, bf16[128,3584]{1,0:T(8,128)(2,1)S(1)}, u32[]{:S(2)}, u32[]{:S(2)}) collective-permute-start(bf16[128,3584]{1,0:T(8,128)(2,1)S(1)} %pad_maximum_fusion.2), channel_id=1, source_target_pairs={{32,0},{33,1},{34,2},{35,3},{36,4},{37,5},{38,6},{39,7},{40,8},{41... | collective-permute-start | bytes 2752520 | tf_op jit(solution)/shard_map/ppermute | solution.py:43
  6.2 14.4 %collective-permute-start.2 = (bf16[64,3584]{1,0:T(8,128)(2,1)S(1)}, bf16[64,3584]{1,0:T(8,128)(2,1)S(1)}, u32[]{:S(2)}, u32[]{:S(2)}) collective-permute-start(bf16[64,3584]{1,0:T(8,128)(2,1)S(1)} %constant_dynamic-slice_fusion.1), channel_id=1, source_target_pairs={{128,0},{129,1},{130,2},{131,3},{132,4},{133,5},{134,6},{135,7},{1... | collective-permute-start | bytes 1376264 | tf_op jit(solution)/shard_map/ppermute | solution.py:43
  11.8 12.0 %collective-permute-start.3 = (bf16[64,3584]{1,0:T(8,128)(2,1)S(1)}, bf16[64,3584]{1,0:T(8,128)(2,1)S(1)}, u32[]{:S(2)}, u32[]{:S(2)}) collective-permute-start(bf16[64,3584]{1,0:T(8,128)(2,1)S(1)} %constant_dynamic-slice_fusion), channel_id=1, source_target_pairs={{134,0},{135,1},{128,2},{129,3},{130,4},{131,5},{132,6},{133,7},{1... | collective-permute-start | bytes 1376264 | tf_op jit(solution)/shard_map/ppermute | solution.py:43
  11.8 21.8 %collective-permute-start.1 = (bf16[128,3584]{1,0:T(8,128)(2,1)S(1)}, bf16[128,3584]{1,0:T(8,128)(2,1)S(1)}, u32[]{:S(2)}, u32[]{:S(2)}) collective-permute-start(bf16[128,3584]{1,0:T(8,128)(2,1)S(1)} %pad_maximum_fusion.2), channel_id=1, source_target_pairs={{96,0},{97,1},{98,2},{99,3},{100,4},{101,5},{102,6},{103,7},{104,8... | collective-permute-start | bytes 2752520 | tf_op jit(solution)/shard_map/ppermute | solution.py:43
  20.7 15.8 %copy-start = (bf16[64,3584]{1,0:T(8,128)(2,1)}, bf16[64,3584]{1,0:T(8,128)(2,1)S(1)}, u32[]{:S(2)}) copy-start(bf16[64,3584]{1,0:T(8,128)(2,1)S(1)} %collective-permute-done.2.refs_5_) | copy-start | bytes 1376260
  23.8 12.7 %copy-start.2 = (bf16[64,3584]{1,0:T(8,128)(2,1)}, bf16[64,3584]{1,0:T(8,128)(2,1)S(1)}, u32[]{:S(2)}) copy-start(bf16[64,3584]{1,0:T(8,128)(2,1)S(1)} %collective-permute-done.3.refs_6_) | copy-start | bytes 1376260
  25.3 16.7 %collective-permute-start.4 = (bf16[96,3584]{1,0:T(8,128)(2,1)S(1)}, bf16[96,3584]{1,0:T(8,128)(2,1)S(1)}, u32[]{:S(2)}, u32[]{:S(2)}) collective-permute-start(bf16[96,3584]{1,0:T(8,128)(2,1)S(1)} %pad_maximum_fusion.4), channel_id=1, source_target_pairs={{32,0},{33,1},{34,2},{35,3},{36,4},{37,5},{38,6},{39,7},{40,8},{41... | collective-permute-start | bytes 2064392 | tf_op jit(solution)/shard_map/ppermute | solution.py:43
  33.7 16.1 %collective-permute-start.5 = (bf16[96,3584]{1,0:T(8,128)(2,1)S(1)}, bf16[96,3584]{1,0:T(8,128)(2,1)S(1)}, u32[]{:S(2)}, u32[]{:S(2)}) collective-permute-start(bf16[96,3584]{1,0:T(8,128)(2,1)S(1)} %pad_maximum_fusion.5), channel_id=1, source_target_pairs={{96,0},{97,1},{98,2},{99,3},{100,4},{101,5},{102,6},{103,7},{104,8... | collective-permute-start | bytes 2064392 | tf_op jit(solution)/shard_map/ppermute | solution.py:43
  33.8 15.9 %collective-permute-start.6 = (bf16[96,3584]{1,0:T(8,128)(2,1)S(1)}, bf16[96,3584]{1,0:T(8,128)(2,1)S(1)}, u32[]{:S(2)}, u32[]{:S(2)}) collective-permute-start(bf16[96,3584]{1,0:T(8,128)(2,1)S(1)} %slice.44), channel_id=1, source_target_pairs={{128,0},{129,1},{130,2},{131,3},{132,4},{133,5},{134,6},{135,7},{1... | collective-permute-start | bytes 2064392 | tf_op jit(solution)/shard_map/ppermute | solution.py:43
  36.4 15.5 %collective-permute-start.7 = (bf16[96,3584]{1,0:T(8,128)(2,1)S(1)}, bf16[96,3584]{1,0:T(8,128)(2,1)S(1)}, u32[]{:S(2)}, u32[]{:S(2)}) collective-permute-start(bf16[96,3584]{1,0:T(8,128)(2,1)S(1)} %slice.45), channel_id=1, source_target_pairs={{134,0},{135,1},{128,2},{129,3},{130,4},{131,5},{132,6},{133,7},{1... | collective-permute-start | bytes 2064392 | tf_op jit(solution)/shard_map/ppermute | solution.py:43
  38.2 44.0 %collective-permute-start.12 = (bf16[384,3584]{1,0:T(8,128)(2,1)}, bf16[384,3584]{1,0:T(8,128)(2,1)}, u32[]{:S(2)}, u32[]{:S(2)}) collective-permute-start(bf16[384,3584]{1,0:T(8,128)(2,1)} %pad_maximum_fusion), channel_id=1, source_target_pairs={{1,0},{0,1},{3,2},{2,3},{5,4},{4,5},{7,6},{6,7},{9,8},{8,9},{11,10... | collective-permute-start | bytes 8257544 | tf_op jit(solution)/shard_map/ppermute | solution.py:43
  49.8 3.9 %copy-start.4 = (bf16[96,3584]{1,0:T(8,128)(2,1)}, bf16[96,3584]{1,0:T(8,128)(2,1)S(1)}, u32[]{:S(2)}) copy-start(bf16[96,3584]{1,0:T(8,128)(2,1)S(1)} %collective-permute-done.6.refs_9_) | copy-start | bytes 2064388
  51.9 1.8 %copy-start.6 = (bf16[96,3584]{1,0:T(8,128)(2,1)}, bf16[96,3584]{1,0:T(8,128)(2,1)S(1)}, u32[]{:S(2)}) copy-start(bf16[96,3584]{1,0:T(8,128)(2,1)S(1)} %collective-permute-done.7.refs_10_) | copy-start | bytes 2064388
  53.7 28.5 %collective-permute-start.13 = (bf16[384,3584]{1,0:T(8,128)(2,1)}, bf16[384,3584]{1,0:T(8,128)(2,1)}, u32[]{:S(2)}, u32[]{:S(2)}) collective-permute-start(bf16[384,3584]{1,0:T(8,128)(2,1)} %pad_maximum_fusion.1), channel_id=1, source_target_pairs={{1,0},{0,1},{3,2},{2,3},{5,4},{4,5},{7,6},{6,7},{9,8},{8,9},{11,10... | collective-permute-start | bytes 8257544 | tf_op jit(solution)/shard_map/ppermute | solution.py:43
  58.0 7.7 %collective-permute-start.8 = (bf16[32,3584]{1,0:T(8,128)(2,1)S(1)}, bf16[32,3584]{1,0:T(8,128)(2,1)S(1)}, u32[]{:S(2)}, u32[]{:S(2)}) collective-permute-start(bf16[32,3584]{1,0:T(8,128)(2,1)S(1)} %get-tuple-element.9), channel_id=1, source_target_pairs={{32,0},{33,1},{34,2},{35,3},{36,4},{37,5},{38,6},{39,7},{40,8},{41... | collective-permute-start | bytes 688136 | tf_op jit(solution)/shard_map/ppermute | solution.py:43
  61.5 11.1 %collective-permute-start.9 = (bf16[32,3584]{1,0:T(8,128)(2,1)}, bf16[32,3584]{1,0:T(8,128)(2,1)}, u32[]{:S(2)}, u32[]{:S(2)}) collective-permute-start(bf16[32,3584]{1,0:T(8,128)(2,1)} %get-tuple-element.7), channel_id=1, source_target_pairs={{96,0},{97,1},{98,2},{99,3},{100,4},{101,5},{102,6},{103,7},{104,8... | collective-permute-start | bytes 688136 | tf_op jit(solution)/shard_map/ppermute | solution.py:43
  61.5 11.1 %collective-permute-start.10 = (bf16[32,3584]{1,0:T(8,128)(2,1)}, bf16[32,3584]{1,0:T(8,128)(2,1)}, u32[]{:S(2)}, u32[]{:S(2)}) collective-permute-start(bf16[32,3584]{1,0:T(8,128)(2,1)} %get-tuple-element.8), channel_id=1, source_target_pairs={{128,0},{129,1},{130,2},{131,3},{132,4},{133,5},{134,6},{135,7},{1... | collective-permute-start | bytes 688136 | tf_op jit(solution)/shard_map/ppermute | solution.py:43
  65.7 7.9 %collective-permute-start.11 = (bf16[32,3584]{1,0:T(8,128)(2,1)}, bf16[32,3584]{1,0:T(8,128)(2,1)}, u32[]{:S(2)}, u32[]{:S(2)}) collective-permute-start(bf16[32,3584]{1,0:T(8,128)(2,1)} %get-tuple-element.6), channel_id=1, source_target_pairs={{134,0},{135,1},{128,2},{129,3},{130,4},{131,5},{132,6},{133,7},{1... | collective-permute-start | bytes 688136 | tf_op jit(solution)/shard_map/ppermute | solution.py:43
  67.9 14.3 %all-to-all-start = ((bf16[8,320,128]{2,1,0:T(8,128)(2,1)}), bf16[8,320,128]{2,1,0:T(8,128)(2,1)}, u32[]{:S(2)}, u32[]{:S(2)}) async-start(bf16[8,320,128]{2,1,0:T(8,128)(2,1)} %bitcast.16), calls=%async_computation | async-start | bytes 1310720 | tf_op jit(solution)/shard_map/all_to_all | solution.py:195
  75.8 6.4 %collective-permute-start.14 = (bf16[128,3584]{1,0:T(8,128)(2,1)}, bf16[128,3584]{1,0:T(8,128)(2,1)}, u32[]{:S(2)}, u32[]{:S(2)}) collective-permute-start(bf16[128,3584]{1,0:T(8,128)(2,1)} %pad_maximum_fusion.3), channel_id=1, source_target_pairs={{1,0},{0,1},{3,2},{2,3},{5,4},{4,5},{7,6},{6,7},{9,8},{8,9},{11,10... | collective-permute-start | bytes 2752520 | tf_op jit(solution)/shard_map/ppermute | solution.py:43
  77.5 34.2 %copy-start.14 = (s32[128]{0:T(128)S(1)}, s32[128]{0:T(128)}, u32[]{:S(2)}) copy-start(s32[128]{0:T(128)} %param.13) | copy-start | bytes 1540
  82.2 1.0 copy-start.1
  83.2 1.0 copy-start.3
  84.2 1.1 copy-start.5
  85.3 1.1 copy-start.7
  86.4 1.2 copy-start.9
  87.6 1.2 copy-start.10
  88.8 1.6 %copy-start.11 = (bf16[320,3584]{1,0:T(8,128)(2,1)S(1)}, bf16[320,3584]{1,0:T(8,128)(2,1)}, u32[]{:S(2)}) copy-start(bf16[320,3584]{1,0:T(8,128)(2,1)} %refs_20_.1) | copy-start | bytes 6881284
  90.4 1.6 %copy-start.12 = (bf16[320,3584]{1,0:T(8,128)(2,1)S(1)}, bf16[320,3584]{1,0:T(8,128)(2,1)}, u32[]{:S(2)}) copy-start(bf16[320,3584]{1,0:T(8,128)(2,1)} %refs_21_.1) | copy-start | bytes 6881284
  105.9 0.8 copy-start.8
  106.7 14.5 %all-to-all-start.1 = ((bf16[8,320,128]{2,1,0:T(8,128)(2,1)}), bf16[8,320,128]{2,1,0:T(8,128)(2,1)S(1)}, u32[]{:S(2)}, u32[]{:S(2)}) async-start(bf16[8,320,128]{2,1,0:T(8,128)(2,1)} %copy-done.8), calls=%async_computation.1 | async-start | bytes 1310720 | tf_op jit(solution)/shard_map/all_to_all | solution.py:198
  121.2 0.9 copy-start.13

commit v2 on v0

v2 whole, which is shorter than its diff:
```python
import functools

import jax
import jax.numpy as jnp
from jax import lax
from jax.experimental import pallas as pl
from jax.experimental.pallas import tpu as pltpu
from jax.sharding import PartitionSpec as P

learn_rate = 0.02
beta_one = 0.9
beta_two = 0.95
epsilon = 1e-08
decay_rate = 0.1

NX, NZL, NY, NZH, NC = 4, 2, 4, 4, 2
NZ = NZL * NZH
N_DP, N_VOCAB = NX * NZL, NY * NZH * NC
TOK = 128
HALF = TOK // 2
CHUNK = 16
ROWS = 320
BLOCK = 512
MIB = 2**20
BF16 = jnp.bfloat16
F32 = jnp.float32


def device_number(x, y, z, core):
    return ((z % NZL) * NX + x) * N_VOCAB + (y * NZH + z // NZL) * NC + core


def receive(value, axes):
    pairs = []
    for x in range(NX):
        for y in range(NY):
            for z in range(NZ):
                for core in range(NC):
                    step = 1 - 2 * core
                    if axes == "core":
                        source = device_number(x, y, z, 1 - core)
                    else:
                        dx, dy, dz = (step if axis in axes else 0 for axis in "xyz")
                        source = device_number((x + dx) % NX, (y + dy) % NY, (z + dz) % NZ, core)
                    pairs.append((source, device_number(x, y, z, core)))
    return lax.ppermute(value, ("dp", "vocab"), pairs)


FIRST, SECOND = 0, 1
OWN, OTHER = 0, 1
HERE, SIDE, ACROSS = 0, 1, 2
CONTENTS = (
    ((0, SIDE, FIRST, OWN), (0, SIDE, FIRST, OTHER)),
    ((1, HERE, FIRST, OWN), (1, HERE, SECOND, OWN)),
    ((0, SIDE, SECOND, OWN), (0, SIDE, SECOND, OTHER)),
    ((1, SIDE, FIRST, OWN), (1, SIDE, FIRST, OTHER)),
    ((0, ACROSS, FIRST, OWN), (1, SIDE, SECOND, OWN)),
    ((0, ACROSS, SECOND, OWN), (1, SIDE, SECOND, OTHER)),
    ((1, ACROSS, FIRST, OWN),),
    ((1, ACROSS, SECOND, OWN),),
)


def pinned(value):
    return pltpu.with_memory_space_constraint(value, pltpu.VMEM)


def in_hbm(value):
    return pltpu.with_memory_space_constraint(value, pltpu.HBM)


VMEM = pl.BlockSpec(memory_space=pltpu.VMEM)
SMEM = pl.BlockSpec(memory_space=pltpu.SMEM)
HBM = pl.BlockSpec(memory_space=pltpu.HBM)
ANY = pl.BlockSpec(memory_space=pl.ANY)


def copy_rows(copies, sem):
    started = []
    for source, at, target, to in copies:
        for row in range(0, HALF, CHUNK):
            started.append(
                pltpu.make_async_copy(
                    source.at[pl.ds(pl.multiple_of(at + row, CHUNK), CHUNK)],
                    target.at[pl.ds(to + row, CHUNK)],
                    sem.at[len(started)],
                )
            )
    for each in started:
        each.start()
    for each in started:
        each.wait()


LATE = (False, False, False, False, False, True, True, True)


def arrange_kernel(place, now_ref, next_ref, x_ref, z_ref, sem):
    core, odd = place[0], place[1]
    own, other = core * HALF, (1 - core) * HALF

    def copy(first_ref, second_ref):
        copy_rows(
            (
                (first_ref, own, x_ref, 0),
                (first_ref, other, x_ref, HALF),
                (first_ref, own, z_ref, 0),
                (second_ref, own, z_ref, HALF),
            ),
            sem,
        )

    @pl.when(odd == 0)
    def _():
        copy(now_ref, next_ref)

    @pl.when(odd == 1)
    def _():
        copy(next_ref, now_ref)


def arrange(place, hidden_now, hidden_next):
    return pl.pallas_call(
        arrange_kernel,
        out_shape=(pltpu.VMEM(hidden_now.shape, BF16),) * 2,
        in_specs=[SMEM, HBM, HBM],
        out_specs=(VMEM,) * 2,
        scratch_shapes=[pltpu.SemaphoreType.DMA((4 * HALF // CHUNK,))],
        compiler_params=pltpu.CompilerParams(vmem_limit_bytes=4 * MIB),
        name="arrange",
    )(place, in_hbm(hidden_now), in_hbm(hidden_next))


EXTRA = 16


def prepare_kernel(cot_ref, target_ref, out_ref):
    turned = cot_ref[...].T
    target = target_ref[...]
    digits = [target // 16384, (target // 128) % 128, target % 128]
    rows = jnp.concatenate(digits + [jnp.zeros((EXTRA - 3, TOK), jnp.int32)], axis=0)
    rows = rows.astype(F32).astype(BF16)
    for g in range(N_DP):
        out_ref[g, :ROWS] = turned[g * ROWS : (g + 1) * ROWS]
        out_ref[g, ROWS:] = rows


def prepare(cotangent, targets):
    return pl.pallas_call(
        prepare_kernel,
        out_shape=jax.ShapeDtypeStruct((N_DP, ROWS + EXTRA, TOK), BF16),
        in_specs=[VMEM, VMEM],
        out_specs=VMEM,
        compiler_params=pltpu.CompilerParams(vmem_limit_bytes=2 * MIB),
        name="prepare",
    )(cotangent, targets.reshape(1, TOK))


def second_round_kernel(x1_ref, z1_ref, x_ref, sem):
    copy_rows(((x1_ref, 0, x_ref, 0), (z1_ref, HALF, x_ref, HALF)), sem)


def third_round_kernel(x2_ref, z2_ref, x_ref, y_ref, z_ref, sem):
    copy_rows(
        ((x2_ref, HALF, x_ref, 0), (x2_ref, 0, y_ref, 0), (z2_ref, HALF, y_ref, HALF), (x2_ref, 0, z_ref, 0)), sem
    )


def rearranged(kernel, values, rows):
    return pl.pallas_call(
        kernel,
        out_shape=tuple(pltpu.VMEM((n, values[0].shape[1]), BF16) for n in rows),
        in_specs=[ANY] * len(values),
        out_specs=(VMEM,) * len(rows),
        scratch_shapes=[pltpu.SemaphoreType.DMA((sum(rows) // CHUNK,))],
        compiler_params=pltpu.CompilerParams(vmem_limit_bytes=2 * MIB),
        name="rearranged",
    )(*values)


def gather(to_x, to_z, cot):
    swap = lambda v: receive(v, "core")
    x1, z1 = receive(to_x, "x"), receive(to_z, "z")
    cot, _, _ = lax.optimization_barrier((cot, x1, z1))
    cot = lax.all_to_all(cot, "dp", 0, 0)
    y2, z2 = receive(x1, "y"), receive(x1, "z")
    (to_x,) = rearranged(second_round_kernel, (x1, z1), (TOK,))
    x2 = receive(to_x, "x")
    y2, z2, x2, cot = lax.optimization_barrier((y2, z2, x2, cot))
    to_x, to_y, to_z = rearranged(third_round_kernel, (x2, z2), (HALF, TOK, HALF))
    y3, z3, x3 = receive(to_y, "y"), receive(to_z, "z"), receive(to_x, "x")
    mine = [x1, z1, y2, z2, x2, y3, z3, x3]
    return mine, [swap(v) for v in mine], cot


def update_kernel(place, now_ref, next_ref, *refs):
    n = 2 * len(CONTENTS)
    pieces, (cot_ref, *state), (out_ref, cot_t, hidden, *kept, total, sems) = refs[:n], refs[n : n + 4], refs[n + 4 :]
    steps = kept[0].shape[1] // BLOCK
    core, odd, dp, vocab = place[0], place[1], place[2], place[3]
    zl, x = dp // NX, lax.rem(dp, NX)
    rank_of = lambda dz, dx: (lax.rem(zl + dz, NZL)) * NX + lax.rem(x + dx, NX)

    copies = [(now_ref, 0, 0, dp * TOK, TOK), (next_ref, 0, 1, dp * TOK, TOK)]
    for group, half in ((0, core), (1, 1 - core)):
        x_at = (0, 1 + 2 * half, 2)
        for number, contents in enumerate(CONTENTS):
            for part, (dz, dx, array, which) in enumerate(contents):
                token = rank_of(dz, x_at[dx]) * TOK + (1 - half if which == OTHER else half) * HALF
                ref = pieces[group * len(CONTENTS) + number]
                copies.append((ref, part * HALF, 1 - odd if array == SECOND else odd, token, HALF))
    columns = lambda step: pl.ds(step * BLOCK, BLOCK)

    for step in range(steps):
        for ref, row, array, token, rows in copies:
            pltpu.make_async_copy(
                ref.at[pl.ds(row, rows), columns(step)],
                hidden.at[array, pl.ds(pl.multiple_of(token, HALF), rows), columns(step)],
                sems.at[step],
            ).start()
        for source, target in zip(state, kept):
            pltpu.make_async_copy(source.at[:, columns(step)], target.at[:, columns(step)], sems.at[step]).start()

    for g in range(N_DP):
        cot_t[:, g * TOK : (g + 1) * TOK] = cot_ref[g, :ROWS]
    for step in range(steps):
        now = hidden.at[:, :, columns(step)]
        pltpu.make_async_copy(now, now, sems.at[step]).wait()
        for target in kept:
            now = target.at[:, columns(step)]
            pltpu.make_async_copy(now, now, sems.at[step]).wait()
        gradient = jnp.dot(cot_t[...], hidden[0, :, columns(step)], preferred_element_type=F32)
        master, moment, second = (target[:, columns(step)].astype(F32) for target in kept)
        moment_new = beta_one * moment + (1.0 - beta_one) * gradient
        second_new = beta_two * second + (1.0 - beta_two) * gradient * gradient
        rows_new = master - learn_rate * (moment_new / (jnp.sqrt(second_new) + epsilon) + decay_rate * master)
        product = lax.dot_general(
            rows_new.astype(BF16), hidden[1, :, columns(step)], (((1,), (1,)), ((), ())), preferred_element_type=F32
        )
        if step == 0:
            total[...] = product
        else:
            total[...] += product

    first_row = vocab * (N_DP * ROWS) + dp * ROWS
    positions = lax.broadcasted_iota(jnp.int32, (ROWS, TOK), 0) + first_row
    for g in range(N_DP):
        logits = total[:, g * TOK : (g + 1) * TOK]
        digits = cot_ref[g, ROWS : ROWS + 3].astype(F32)
        target = (digits[0:1] * 16384.0 + digits[1:2] * 128.0 + digits[2:3]).astype(jnp.int32)
        top = jnp.max(logits, axis=0, keepdims=True)
        sums = jnp.sum(jnp.exp(logits - top), axis=0, keepdims=True)
        picked = jnp.sum(jnp.where(positions == target, logits, 0.0), axis=0, keepdims=True)
        rest = jnp.concatenate([top, sums, picked], axis=0)
        rows = []
        for _ in range(3):
            rows.append(rest.astype(BF16).astype(F32))
            rest = rest - rows[-1]
        rows.append(jnp.zeros((EXTRA - 9, TOK), F32))
        out_ref[g, :ROWS] = logits.astype(BF16)
        out_ref[g, ROWS:] = jnp.concatenate(rows, axis=0).astype(BF16)


def update_and_logits(place, now_next, mine, other, cot, state):
    whole = (N_DP, ROWS + EXTRA, TOK)
    placed = [pinned(v) if late else in_hbm(v) for values in (mine, other) for v, late in zip(values, LATE)]
    width = state[0].shape[1]
    return pl.pallas_call(
        update_kernel,
        out_shape=jax.ShapeDtypeStruct(whole, BF16),
        in_specs=[SMEM, HBM, HBM] + [ANY] * (len(mine) + len(other)) + [VMEM] + [HBM] * 3,
        out_specs=VMEM,
        scratch_shapes=[
            pltpu.VMEM((ROWS, N_DP * TOK), BF16),
            pltpu.VMEM((2, N_DP * TOK, width), BF16),
            *[pltpu.VMEM(v.shape, v.dtype) for v in state],
            pltpu.VMEM((ROWS, N_DP * TOK), F32),
            pltpu.SemaphoreType.DMA((width // BLOCK,)),
        ],
        compiler_params=pltpu.CompilerParams(vmem_limit_bytes=32 * MIB),
        cost_estimate=pl.CostEstimate(flops=9_400_000_000, bytes_accessed=24_000_000, transcendentals=2_300_000),
        name="update_and_logits",
    )(place, *[in_hbm(v) for v in now_next], *placed, cot, *[in_hbm(v) for v in state])


def turn_kernel(part_ref, out_ref):
    rows = jnp.concatenate([part_ref[g, :ROWS] for g in range(N_DP)], axis=0)
    out_ref[...] = rows.T


def turn(parts):
    return pl.pallas_call(
        turn_kernel,
        out_shape=jax.ShapeDtypeStruct((TOK, N_DP * ROWS), BF16),
        in_specs=[VMEM],
        out_specs=VMEM,
        compiler_params=pltpu.CompilerParams(vmem_limit_bytes=4 * MIB),
        cost_estimate=pl.CostEstimate(flops=0, bytes_accessed=1_400_000, transcendentals=0),
        name="turn",
    )(parts)


def merged(value):
    top, sums, picked = value[:, 0], value[:, 1], value[:, 2]
    row_top = jnp.max(top, axis=0, keepdims=True)
    row_total = jnp.sum(sums * jnp.exp(top - row_top), axis=0, keepdims=True)
    return row_top, row_total, jnp.sum(picked, axis=0, keepdims=True)


def merge_kernel(part_ref, out_ref, extra, sem):
    load = pltpu.make_async_copy(part_ref.at[:, pl.ds(ROWS, EXTRA), :], extra, sem)
    load.start()
    load.wait()
    rows = extra[...].astype(F32)
    value = rows[:, 0:3] + rows[:, 3:6] + rows[:, 6:9]
    out_ref[...] = jnp.broadcast_to(jnp.concatenate(merged(value), axis=0)[None], out_ref.shape)


def merge(parts):
    return pl.pallas_call(
        merge_kernel,
        out_shape=jax.ShapeDtypeStruct((N_VOCAB, 3, TOK), F32),
        in_specs=[ANY],
        out_specs=VMEM,
        scratch_shapes=[pltpu.VMEM((N_DP, EXTRA, TOK), BF16), pltpu.SemaphoreType.DMA(())],
        compiler_params=pltpu.CompilerParams(vmem_limit_bytes=4 * MIB),
        name="merge",
    )(parts)


def loss_kernel(stat_ref, out_ref):
    row_top, row_total, picked = merged(stat_ref[...])
    out_ref[...] = jnp.log(row_total) + row_top - picked


def loss(stat):
    out = pl.pallas_call(
        loss_kernel,
        out_shape=jax.ShapeDtypeStruct((1, TOK), F32),
        in_specs=[VMEM],
        out_specs=VMEM,
        compiler_params=pltpu.CompilerParams(vmem_limit_bytes=4 * MIB),
        name="loss",
    )(stat)
    return out.reshape(TOK)


def shards(hidden_now, hidden_next, cotangent, master, moment, second, targets):
    dp, vocab = lax.axis_index("dp"), lax.axis_index("vocab")
    place = jnp.stack([vocab % NC, (vocab // (NZH * NC)) % 2, dp, vocab]).astype(jnp.int32)
    to_x, to_z = arrange(place, hidden_now, hidden_next)
    mine, other, cot = gather(to_x, to_z, prepare(cotangent, targets))
    parts = update_and_logits(place, (hidden_now, hidden_next), mine, other, cot, (master, moment, second))
    parts = lax.all_to_all(parts, "dp", 0, 0)
    stat = lax.all_to_all(merge(parts), "vocab", 0, 0)
    return turn(parts), loss(stat)


def solution(mesh):
    in_specs = (
        P("dp", None),
        P("dp", None),
        P("dp", "vocab"),
        P(("vocab", "dp"), None),
        P(("vocab", "dp"), None),
        P(("vocab", "dp"), None),
        P("dp"),
    )
    out_specs = (P("dp", "vocab"), P("dp"))
    return jax.shard_map(shards, mesh=mesh, in_specs=in_specs, out_specs=out_specs, check_vma=False)
```

time: 468 us -> 114 us (0.24)
  waiting for transfers between devices: 281 us -> 36.3 us
  blocking collectives: 145 us -> 15.4 us
  starting transfers between devices: 3.62 us -> 39.8 us
  Pallas kernels: 0 us -> 20.8 us
  matrix products: 20.7 us -> 0 us
  between operations: 14.1 us -> 0.79 us
    reduce_scatter x1 -> x0, waiting for transfers between devices: 190 us -> none  [shards(): lax.psum_scatter(partial_grad.astype(jnp.bfloat16), 'dp', scatter_dimensi...]
    all_gather x1 -> x0, waiting for transfers between devices: 79.9 us -> none  [shards(): lax.all_gather(hidden_next, 'dp', axis=0, tiled=True)]
    psum x1 -> x0, blocking collectives: 73.8 us -> none  [shards(): row_total, target_logit = lax.psum((local_total, picked), 'vocab')]
    pmax x1 -> x0, blocking collectives: 70.8 us -> none  [shards(): row_top = lax.pmax(jnp.max(logits, axis=1), 'vocab')]
    ppermute x0 -> x16, starting transfers between devices: none -> 28.9 us  [receive(): return lax.ppermute(value, ('dp', 'vocab'), pairs)]
    ppermute x0 -> x16, waiting for transfers between devices: none -> 27.6 us  [receive(): return lax.ppermute(value, ('dp', 'vocab'), pairs)]
    pallas_call x0 -> x8, Pallas kernels: none -> 20.8 us  [the longest x1 11 us: update_and_logits(): pl.pallas_call(update_kernel, out_shape=jax.ShapeDtypeStruct(whole, BF16)...]
    dot_general x2 -> x0, matrix products: 20.7 us -> none  [the longest x1 10.7 us: shards(): lax.dot_general(lax.all_gather(hidden_next, 'dp', axis=0, tiled=True), he...]
  transfers between devices with their start and end apart: 3 -> 18, of which waited for: 3 -> 9; matrix products, arithmetic and copies ran while one was open for 2% -> 0% of each run, Pallas kernels for 0% -> 6%
where the time goes in v2:
time: 114 us
  starting transfers between devices  39.8 us (35%)
  waiting for transfers between devices  36.3 us (32%)
  Pallas kernels  20.8 us (18%)
  blocking collectives  15.4 us (14%)
    ppermute x16, starting transfers between devices, receive(): return lax.ppermute(value, ('dp', 'vocab'), pairs)  28.9 us
    ppermute x16, waiting for transfers between devices, receive(): return lax.ppermute(value, ('dp', 'vocab'), pairs)  27.6 us
    all_to_all x1, blocking collectives, shards(): parts = lax.all_to_all(parts, 'dp', 0, 0)  15.4 us
    pallas_call x1, Pallas kernels, update_and_logits(): pl.pallas_call(update_kernel, out_shape=jax.ShapeDtypeStruct(whole, BF16)...  11 us
    all_to_all x1, waiting for transfers between devices, shards(): stat = lax.all_to_all(merge(parts), 'vocab', 0, 0)  8.69 us
    all_to_all x1, starting transfers between devices, shards(): stat = lax.all_to_all(merge(parts), 'vocab', 0, 0)  7.1 us
    pallas_call x2, Pallas kernels, rearranged(): pl.pallas_call(kernel, out_shape=tuple((pltpu.VMEM((n, values[0].shape[1]...  4.21 us
    all_to_all x1, starting transfers between devices, gather(): cot = lax.all_to_all(cot, 'dp', 0, 0)  3.73 us
  transfers between devices with their start and end apart: 18, of which 9 were waited for; matrix products, arithmetic and copies ran while one was open for 0% of the time, Pallas kernels for 6%

profile of v2, /device:TPU:1, one launch (start us, length us, event | category | flops | bytes accessed | tf_op | source)
XLA Modules:
  0.0 113.9 jit_solution(12972780965071338398)
XLA Ops:
  0.8 2.2 %arrange.1 = (bf16[128,3584]{1,0:T(8,128)(2,1)S(1)}, bf16[128,3584]{1,0:T(8,128)(2,1)S(1)}) custom-call(s32[4]{0:T(128)S(1)} %pad_add_fusion.place, bf16[128,3584]{1,0:T(8,128)(2,1)} %now_ref.3, bf16[128,3584]{1,0:T(8,128)(2,1)} %next_ref.3), custom_call_target="tpu_custom_call" | custom-call | tf_op jit(solution)/shard_map/arrange/pallas_call | solution.py:123
  3.0 2.1 %collective-permute-start = (bf16[128,3584]{1,0:T(8,128)(2,1)S(1)}, bf16[128,3584]{1,0:T(8,128)(2,1)S(1)}, u32[]{:S(2)}, u32[]{:S(2)}) collective-permute-start(bf16[128,3584]{1,0:T(8,128)(2,1)S(1)} %get-tuple-element.12), channel_id=1, source_target_pairs={{32,0},{97,1},{160,128},{225,129},{34,2},{99,3},{162,130},{227,131... | collective-permute-start | bytes 2752520 | tf_op jit(solution)/shard_map/ppermute | solution.py:46
  5.1 1.6 %collective-permute-start.1 = (bf16[128,3584]{1,0:T(8,128)(2,1)S(1)}, bf16[128,3584]{1,0:T(8,128)(2,1)}, u32[]{:S(2)}, u32[]{:S(2)}) collective-permute-start(bf16[128,3584]{1,0:T(8,128)(2,1)S(1)} %get-tuple-element.13), channel_id=1, source_target_pairs={{128,0},{135,1},{2,128},{1,129},{130,2},{129,3},{4,130},{3,131},{1... | collective-permute-start | bytes 2752520 | tf_op jit(solution)/shard_map/ppermute | solution.py:46
  6.7 0.7 copy-done.4
  7.4 1.1 prepare.1
  8.5 8.7 %collective-permute-done.x1_ref.refs_0_ = bf16[128,3584]{1,0:T(8,128)(2,1)S(1)} collective-permute-done((bf16[128,3584]{1,0:T(8,128)(2,1)S(1)}, bf16[128,3584]{1,0:T(8,128)(2,1)S(1)}, u32[]{:S(2)}, u32[]{:S(2)}) %collective-permute-start) | collective-permute-done | bytes 917536 | tf_op jit(solution)/shard_map/ppermute | solution.py:46
  17.1 4.4 %collective-permute-done.1.z1_ref.refs_1_ = bf16[128,3584]{1,0:T(8,128)(2,1)} collective-permute-done((bf16[128,3584]{1,0:T(8,128)(2,1)S(1)}, bf16[128,3584]{1,0:T(8,128)(2,1)}, u32[]{:S(2)}, u32[]{:S(2)}) %collective-permute-start.1) | collective-permute-done | bytes 917536 | tf_op jit(solution)/shard_map/ppermute | solution.py:46
  21.6 3.7 %all-to-all-start = ((bf16[8,336,128]{2,1,0:T(8,128)(2,1)}), bf16[8,336,128]{2,1,0:T(8,128)(2,1)S(1)}, u32[]{:S(2)}, u32[]{:S(2)}) async-start(bf16[8,336,128]{2,1,0:T(8,128)(2,1)} %prepare.1), calls=%async_computation | async-start | bytes 1376256 | tf_op jit(solution)/shard_map/all_to_all | solution.py:185
  25.3 1.5 %collective-permute-start.3 = (bf16[128,3584]{1,0:T(8,128)(2,1)S(1)}, bf16[128,3584]{1,0:T(8,128)(2,1)S(1)}, u32[]{:S(2)}, u32[]{:S(2)}) collective-permute-start(bf16[128,3584]{1,0:T(8,128)(2,1)S(1)} %collective-permute-done.x1_ref.refs_0_), channel_id=1, source_target_pairs={{128,0},{135,1},{2,128},{1,129},{130,2},{129,3},{4,130},{3,131},{1... | collective-permute-start | bytes 2752520 | tf_op jit(solution)/shard_map/ppermute | solution.py:46
  26.7 1.3 %collective-permute-start.2 = (bf16[128,3584]{1,0:T(8,128)(2,1)S(1)}, bf16[128,3584]{1,0:T(8,128)(2,1)}, u32[]{:S(2)}, u32[]{:S(2)}) collective-permute-start(bf16[128,3584]{1,0:T(8,128)(2,1)S(1)} %collective-permute-done.x1_ref.refs_0_), channel_id=1, source_target_pairs={{8,0},{25,1},{136,128},{153,129},{10,2},{27,3},{138,130},{155,131}... | collective-permute-start | bytes 2752520 | tf_op jit(solution)/shard_map/ppermute | solution.py:46
  28.1 1.7 %rearranged.2 = bf16[128,3584]{1,0:T(8,128)(2,1)S(1)} custom-call(bf16[128,3584]{1,0:T(8,128)(2,1)S(1)} %collective-permute-done.x1_ref.refs_0_, bf16[128,3584]{1,0:T(8,128)(2,1)} %collective-permute-done.1.z1_ref.refs_1_), custom_call_target="tpu_custom_call" | custom-call | tf_op jit(solution)/shard_map/rearranged/pallas_call | solution.py:170
  29.8 1.3 %collective-permute-start.4 = (bf16[128,3584]{1,0:T(8,128)(2,1)S(1)}, bf16[128,3584]{1,0:T(8,128)(2,1)S(1)}, u32[]{:S(2)}, u32[]{:S(2)}) collective-permute-start(bf16[128,3584]{1,0:T(8,128)(2,1)S(1)} %rearranged.2), channel_id=1, source_target_pairs={{32,0},{97,1},{160,128},{225,129},{34,2},{99,3},{162,130},{227,131... | collective-permute-start | bytes 2752520 | tf_op jit(solution)/shard_map/ppermute | solution.py:46
  31.0 7.9 %collective-permute-start.8 = (bf16[128,3584]{1,0:T(8,128)(2,1)S(1)}, bf16[128,3584]{1,0:T(8,128)(2,1)}, u32[]{:S(2)}, u32[]{:S(2)}) collective-permute-start(bf16[128,3584]{1,0:T(8,128)(2,1)S(1)} %collective-permute-done.x1_ref.refs_0_), channel_id=1, source_target_pairs={{1,0},{0,1},{129,128},{128,129},{3,2},{2,3},{131,130},{130,131},{5... | collective-permute-start | bytes 2752520 | tf_op jit(solution)/shard_map/ppermute | solution.py:46
  39.0 4.3 %collective-permute-done.3.z2_ref.refs_3_ = bf16[128,3584]{1,0:T(8,128)(2,1)S(1)} collective-permute-done((bf16[128,3584]{1,0:T(8,128)(2,1)S(1)}, bf16[128,3584]{1,0:T(8,128)(2,1)S(1)}, u32[]{:S(2)}, u32[]{:S(2)}) %collective-permute-start.3) | collective-permute-done | bytes 917536 | tf_op jit(solution)/shard_map/ppermute | solution.py:46
  43.3 3.4 %collective-permute-done.4.x2_ref.refs_4_ = bf16[128,3584]{1,0:T(8,128)(2,1)S(1)} collective-permute-done((bf16[128,3584]{1,0:T(8,128)(2,1)S(1)}, bf16[128,3584]{1,0:T(8,128)(2,1)S(1)}, u32[]{:S(2)}, u32[]{:S(2)}) %collective-permute-start.4) | collective-permute-done | bytes 917536 | tf_op jit(solution)/shard_map/ppermute | solution.py:46
  46.6 2.5 %rearranged.3 = (bf16[64,3584]{1,0:T(8,128)(2,1)S(1)}, bf16[128,3584]{1,0:T(8,128)(2,1)S(1)}, bf16[64,3584]{1,0:T(8,128)(2,1)S(1)}) custom-call(bf16[128,3584]{1,0:T(8,128)(2,1)S(1)} %collective-permute-done.4.x2_ref.refs_4_, bf16[128,3584]{1,0:T(8,128)(2,1)S(1)} %collective-permute-done.3.z2_ref.refs_3_), custom_call_target="tpu_custom_call" | custom-call | tf_op jit(solution)/shard_map/rearranged/pallas_call | solution.py:170
  49.2 1.4 %collective-permute-start.5 = (bf16[128,3584]{1,0:T(8,128)(2,1)S(1)}, bf16[128,3584]{1,0:T(8,128)(2,1)S(1)}, u32[]{:S(2)}, u32[]{:S(2)}) collective-permute-start(bf16[128,3584]{1,0:T(8,128)(2,1)S(1)} %get-tuple-element.18), channel_id=1, source_target_pairs={{8,0},{25,1},{136,128},{153,129},{10,2},{27,3},{138,130},{155,131}... | collective-permute-start | bytes 2752520 | tf_op jit(solution)/shard_map/ppermute | solution.py:46
  50.6 0.9 collective-permute-start.6
  51.5 2.9 %collective-permute-start.10 = (bf16[128,3584]{1,0:T(8,128)(2,1)}, bf16[128,3584]{1,0:T(8,128)(2,1)S(1)}, u32[]{:S(2)}, u32[]{:S(2)}) collective-permute-start(bf16[128,3584]{1,0:T(8,128)(2,1)} %collective-permute-done.2.refs_2_), channel_id=1, source_target_pairs={{1,0},{0,1},{129,128},{128,129},{3,2},{2,3},{131,130},{130,131},{5... | collective-permute-start | bytes 2752520 | tf_op jit(solution)/shard_map/ppermute | solution.py:46
  54.4 1.8 %collective-permute-start.7 = (bf16[64,3584]{1,0:T(8,128)(2,1)S(1)}, bf16[64,3584]{1,0:T(8,128)(2,1)S(1)}, u32[]{:S(2)}, u32[]{:S(2)}) collective-permute-start(bf16[64,3584]{1,0:T(8,128)(2,1)S(1)} %get-tuple-element.20), channel_id=1, source_target_pairs={{32,0},{97,1},{160,128},{225,129},{34,2},{99,3},{162,130},{227,131... | collective-permute-start | bytes 1376264 | tf_op jit(solution)/shard_map/ppermute | solution.py:46
  56.2 2.9 %collective-permute-done.6.refs_6_ = bf16[64,3584]{1,0:T(8,128)(2,1)S(1)} collective-permute-done((bf16[64,3584]{1,0:T(8,128)(2,1)S(1)}, bf16[64,3584]{1,0:T(8,128)(2,1)S(1)}, u32[]{:S(2)}, u32[]{:S(2)}) %collective-permute-start.6) | collective-permute-done | bytes 458784 | tf_op jit(solution)/shard_map/ppermute | solution.py:46
  59.1 2.6 %collective-permute-start.12 = (bf16[128,3584]{1,0:T(8,128)(2,1)S(1)}, bf16[128,3584]{1,0:T(8,128)(2,1)S(1)}, u32[]{:S(2)}, u32[]{:S(2)}) collective-permute-start(bf16[128,3584]{1,0:T(8,128)(2,1)S(1)} %collective-permute-done.4.x2_ref.refs_4_), channel_id=1, source_target_pairs={{1,0},{0,1},{129,128},{128,129},{3,2},{2,3},{131,130},{130,131},{5... | collective-permute-start | bytes 2752520 | tf_op jit(solution)/shard_map/ppermute | solution.py:46
  61.7 1.1 collective-permute-done.5.refs_5_
  62.8 3.1 %collective-permute-start.13 = (bf16[128,3584]{1,0:T(8,128)(2,1)S(1)}, bf16[128,3584]{1,0:T(8,128)(2,1)S(1)}, u32[]{:S(2)}, u32[]{:S(2)}) collective-permute-start(bf16[128,3584]{1,0:T(8,128)(2,1)S(1)} %collective-permute-done.5.refs_5_), channel_id=1, source_target_pairs={{1,0},{0,1},{129,128},{128,129},{3,2},{2,3},{131,130},{130,131},{5... | collective-permute-start | bytes 2752520 | tf_op jit(solution)/shard_map/ppermute | solution.py:46
  66.4 2.2 %collective-permute-done.14.refs_14_ = bf16[64,3584]{1,0:T(8,128)(2,1)S(1)} collective-permute-done((bf16[64,3584]{1,0:T(8,128)(2,1)S(1)}, bf16[64,3584]{1,0:T(8,128)(2,1)S(1)}, u32[]{:S(2)}, u32[]{:S(2)}) %collective-permute-start.14) | collective-permute-done | bytes 458784 | tf_op jit(solution)/shard_map/ppermute | solution.py:46
  68.6 0.7 collective-permute-done.15.refs_15_
  69.3 11.0 %update_and_logits.1 = bf16[8,336,128]{2,1,0:T(8,128)(2,1)S(1)} custom-call(s32[4]{0:T(128)S(1)} %pad_add_fusion.place, bf16[128,3584]{1,0:T(8,128)(2,1)} %now_ref.3, bf16[128,3584]{1,0:T(8,128)(2,1)} %next_ref.3, bf16[128,3584]{1,0:T(8,128)(2,1)} %copy-done.2, bf16[128,3584]{1,0:T(8,128)(2,1)} %collective-permute-done.1.z1_ref.refs_1_, ...), custom_call_target="tpu_custom_call" | custom-call | flops 9400000512 | bytes 24000000 | tf_op jit(solution)/shard_map/update_and_logits/pallas_call | solution.py:268
  80.3 15.4 %all_to_all.15.part_ref = bf16[8,336,128]{2,1,0:T(8,128)(2,1)S(1)} all-to-all(bf16[8,336,128]{2,1,0:T(8,128)(2,1)S(1)} %update_and_logits.1), channel_id=1, replica_groups=mesh['dp'=8,'vocab'=32] {'dp'}, dimensions={0} | all-to-all | bytes 1376256 | tf_op jit(solution)/shard_map/all_to_all | solution.py:354
  95.8 0.7 merge.1
  96.4 7.1 %all-to-all-start.2 = ((f32[32,3,128]{2,1,0:T(4,128)}), f32[32,3,128]{2,1,0:T(4,128)S(1)}, u32[]{:S(2)}, u32[]{:S(2)}) async-start(f32[32,3,128]{2,1,0:T(4,128)} %merge.1), calls=%async_computation.2 | async-start | bytes 131072 | tf_op jit(solution)/shard_map/all_to_all | solution.py:355
  103.6 1.1 turn.1
  104.6 8.7 %all-to-all-done.2.stat_ref = f32[32,3,128]{2,1,0:T(4,128)S(1)} async-done(((f32[32,3,128]{2,1,0:T(4,128)}), f32[32,3,128]{2,1,0:T(4,128)S(1)}, u32[]{:S(2)}, u32[]{:S(2)}) %all-to-all-start.2) | async-done | bytes 49184 | tf_op jit(solution)/shard_map/all_to_all | solution.py:355
  (30 shorter events, 1.2 us)
Async XLA Ops:
  0.6 6.1 %copy-start.3 = (bf16[128,2560]{1,0:T(8,128)(2,1)S(1)}, bf16[128,2560]{1,0:T(8,128)(2,1)}, u32[]{:S(2)}) copy-start(bf16[128,2560]{1,0:T(8,128)(2,1)} %cot_ref.1) | copy-start | bytes 1966084
  3.0 14.2 %collective-permute-start = (bf16[128,3584]{1,0:T(8,128)(2,1)S(1)}, bf16[128,3584]{1,0:T(8,128)(2,1)S(1)}, u32[]{:S(2)}, u32[]{:S(2)}) collective-permute-start(bf16[128,3584]{1,0:T(8,128)(2,1)S(1)} %get-tuple-element.12), channel_id=1, source_target_pairs={{32,0},{97,1},{160,128},{225,129},{34,2},{99,3},{162,130},{227,131... | collective-permute-start | bytes 2752520 | tf_op jit(solution)/shard_map/ppermute | solution.py:46
  5.1 16.5 %collective-permute-start.1 = (bf16[128,3584]{1,0:T(8,128)(2,1)S(1)}, bf16[128,3584]{1,0:T(8,128)(2,1)}, u32[]{:S(2)}, u32[]{:S(2)}) collective-permute-start(bf16[128,3584]{1,0:T(8,128)(2,1)S(1)} %get-tuple-element.13), channel_id=1, source_target_pairs={{128,0},{135,1},{2,128},{1,129},{130,2},{129,3},{4,130},{3,131},{1... | collective-permute-start | bytes 2752520 | tf_op jit(solution)/shard_map/ppermute | solution.py:46
  6.7 0.7 copy-start.4
  17.1 32.0 %copy-start.2 = (bf16[128,3584]{1,0:T(8,128)(2,1)}, bf16[128,3584]{1,0:T(8,128)(2,1)S(1)}, u32[]{:S(2)}) copy-start(bf16[128,3584]{1,0:T(8,128)(2,1)S(1)} %collective-permute-done.x1_ref.refs_0_) | copy-start | bytes 2752516
  21.6 25.1 %all-to-all-start = ((bf16[8,336,128]{2,1,0:T(8,128)(2,1)}), bf16[8,336,128]{2,1,0:T(8,128)(2,1)S(1)}, u32[]{:S(2)}, u32[]{:S(2)}) async-start(bf16[8,336,128]{2,1,0:T(8,128)(2,1)} %prepare.1), calls=%async_computation | async-start | bytes 1376256 | tf_op jit(solution)/shard_map/all_to_all | solution.py:185
  25.3 18.0 %collective-permute-start.3 = (bf16[128,3584]{1,0:T(8,128)(2,1)S(1)}, bf16[128,3584]{1,0:T(8,128)(2,1)S(1)}, u32[]{:S(2)}, u32[]{:S(2)}) collective-permute-start(bf16[128,3584]{1,0:T(8,128)(2,1)S(1)} %collective-permute-done.x1_ref.refs_0_), channel_id=1, source_target_pairs={{128,0},{135,1},{2,128},{1,129},{130,2},{129,3},{4,130},{3,131},{1... | collective-permute-start | bytes 2752520 | tf_op jit(solution)/shard_map/ppermute | solution.py:46
  26.7 16.5 %collective-permute-start.2 = (bf16[128,3584]{1,0:T(8,128)(2,1)S(1)}, bf16[128,3584]{1,0:T(8,128)(2,1)}, u32[]{:S(2)}, u32[]{:S(2)}) collective-permute-start(bf16[128,3584]{1,0:T(8,128)(2,1)S(1)} %collective-permute-done.x1_ref.refs_0_), channel_id=1, source_target_pairs={{8,0},{25,1},{136,128},{153,129},{10,2},{27,3},{138,130},{155,131}... | collective-permute-start | bytes 2752520 | tf_op jit(solution)/shard_map/ppermute | solution.py:46
  29.8 16.8 %collective-permute-start.4 = (bf16[128,3584]{1,0:T(8,128)(2,1)S(1)}, bf16[128,3584]{1,0:T(8,128)(2,1)S(1)}, u32[]{:S(2)}, u32[]{:S(2)}) collective-permute-start(bf16[128,3584]{1,0:T(8,128)(2,1)S(1)} %rearranged.2), channel_id=1, source_target_pairs={{32,0},{97,1},{160,128},{225,129},{34,2},{99,3},{162,130},{227,131... | collective-permute-start | bytes 2752520 | tf_op jit(solution)/shard_map/ppermute | solution.py:46
  31.0 23.4 %collective-permute-start.8 = (bf16[128,3584]{1,0:T(8,128)(2,1)S(1)}, bf16[128,3584]{1,0:T(8,128)(2,1)}, u32[]{:S(2)}, u32[]{:S(2)}) collective-permute-start(bf16[128,3584]{1,0:T(8,128)(2,1)S(1)} %collective-permute-done.x1_ref.refs_0_), channel_id=1, source_target_pairs={{1,0},{0,1},{129,128},{128,129},{3,2},{2,3},{131,130},{130,131},{5... | collective-permute-start | bytes 2752520 | tf_op jit(solution)/shard_map/ppermute | solution.py:46
  39.0 15.5 %collective-permute-start.9 = (bf16[128,3584]{1,0:T(8,128)(2,1)}, bf16[128,3584]{1,0:T(8,128)(2,1)}, u32[]{:S(2)}, u32[]{:S(2)}) collective-permute-start(bf16[128,3584]{1,0:T(8,128)(2,1)} %collective-permute-done.1.z1_ref.refs_1_), channel_id=1, source_target_pairs={{1,0},{0,1},{129,128},{128,129},{3,2},{2,3},{131,130},{130,131},{5... | collective-permute-start | bytes 2752520 | tf_op jit(solution)/shard_map/ppermute | solution.py:46
  43.2 26.1 %copy-start = (bf16[128,3584]{1,0:T(8,128)(2,1)}, bf16[128,3584]{1,0:T(8,128)(2,1)S(1)}, u32[]{:S(2)}) copy-start(bf16[128,3584]{1,0:T(8,128)(2,1)S(1)} %collective-permute-done.3.z2_ref.refs_3_) | copy-start | bytes 2752516
  46.6 22.7 %copy-start.1 = (bf16[128,3584]{1,0:T(8,128)(2,1)}, bf16[128,3584]{1,0:T(8,128)(2,1)S(1)}, u32[]{:S(2)}) copy-start(bf16[128,3584]{1,0:T(8,128)(2,1)S(1)} %collective-permute-done.4.x2_ref.refs_4_) | copy-start | bytes 2752516
  49.2 13.6 %collective-permute-start.5 = (bf16[128,3584]{1,0:T(8,128)(2,1)S(1)}, bf16[128,3584]{1,0:T(8,128)(2,1)S(1)}, u32[]{:S(2)}, u32[]{:S(2)}) collective-permute-start(bf16[128,3584]{1,0:T(8,128)(2,1)S(1)} %get-tuple-element.18), channel_id=1, source_target_pairs={{8,0},{25,1},{136,128},{153,129},{10,2},{27,3},{138,130},{155,131}... | collective-permute-start | bytes 2752520 | tf_op jit(solution)/shard_map/ppermute | solution.py:46
  50.6 8.5 %collective-permute-start.6 = (bf16[64,3584]{1,0:T(8,128)(2,1)S(1)}, bf16[64,3584]{1,0:T(8,128)(2,1)S(1)}, u32[]{:S(2)}, u32[]{:S(2)}) collective-permute-start(bf16[64,3584]{1,0:T(8,128)(2,1)S(1)} %get-tuple-element.19), channel_id=1, source_target_pairs={{128,0},{135,1},{2,128},{1,129},{130,2},{129,3},{4,130},{3,131},{1... | collective-permute-start | bytes 1376264 | tf_op jit(solution)/shard_map/ppermute | solution.py:46
  51.5 14.4 %collective-permute-start.10 = (bf16[128,3584]{1,0:T(8,128)(2,1)}, bf16[128,3584]{1,0:T(8,128)(2,1)S(1)}, u32[]{:S(2)}, u32[]{:S(2)}) collective-permute-start(bf16[128,3584]{1,0:T(8,128)(2,1)} %collective-permute-done.2.refs_2_), channel_id=1, source_target_pairs={{1,0},{0,1},{129,128},{128,129},{3,2},{2,3},{131,130},{130,131},{5... | collective-permute-start | bytes 2752520 | tf_op jit(solution)/shard_map/ppermute | solution.py:46
  54.4 12.0 %collective-permute-start.11 = (bf16[128,3584]{1,0:T(8,128)(2,1)S(1)}, bf16[128,3584]{1,0:T(8,128)(2,1)S(1)}, u32[]{:S(2)}, u32[]{:S(2)}) collective-permute-start(bf16[128,3584]{1,0:T(8,128)(2,1)S(1)} %collective-permute-done.3.z2_ref.refs_3_), channel_id=1, source_target_pairs={{1,0},{0,1},{129,128},{128,129},{3,2},{2,3},{131,130},{130,131},{5... | collective-permute-start | bytes 2752520 | tf_op jit(solution)/shard_map/ppermute | solution.py:46
  54.4 11.5 %collective-permute-start.7 = (bf16[64,3584]{1,0:T(8,128)(2,1)S(1)}, bf16[64,3584]{1,0:T(8,128)(2,1)S(1)}, u32[]{:S(2)}, u32[]{:S(2)}) collective-permute-start(bf16[64,3584]{1,0:T(8,128)(2,1)S(1)} %get-tuple-element.20), channel_id=1, source_target_pairs={{32,0},{97,1},{160,128},{225,129},{34,2},{99,3},{162,130},{227,131... | collective-permute-start | bytes 1376264 | tf_op jit(solution)/shard_map/ppermute | solution.py:46
  59.1 7.3 %collective-permute-start.12 = (bf16[128,3584]{1,0:T(8,128)(2,1)S(1)}, bf16[128,3584]{1,0:T(8,128)(2,1)S(1)}, u32[]{:S(2)}, u32[]{:S(2)}) collective-permute-start(bf16[128,3584]{1,0:T(8,128)(2,1)S(1)} %collective-permute-done.4.x2_ref.refs_4_), channel_id=1, source_target_pairs={{1,0},{0,1},{129,128},{128,129},{3,2},{2,3},{131,130},{130,131},{5... | collective-permute-start | bytes 2752520 | tf_op jit(solution)/shard_map/ppermute | solution.py:46
  62.8 6.5 %collective-permute-start.13 = (bf16[128,3584]{1,0:T(8,128)(2,1)S(1)}, bf16[128,3584]{1,0:T(8,128)(2,1)S(1)}, u32[]{:S(2)}, u32[]{:S(2)}) collective-permute-start(bf16[128,3584]{1,0:T(8,128)(2,1)S(1)} %collective-permute-done.5.refs_5_), channel_id=1, source_target_pairs={{1,0},{0,1},{129,128},{128,129},{3,2},{2,3},{131,130},{130,131},{5... | collective-permute-start | bytes 2752520 | tf_op jit(solution)/shard_map/ppermute | solution.py:46
  65.9 2.8 %collective-permute-start.14 = (bf16[64,3584]{1,0:T(8,128)(2,1)S(1)}, bf16[64,3584]{1,0:T(8,128)(2,1)S(1)}, u32[]{:S(2)}, u32[]{:S(2)}) collective-permute-start(bf16[64,3584]{1,0:T(8,128)(2,1)S(1)} %collective-permute-done.6.refs_6_), channel_id=1, source_target_pairs={{1,0},{0,1},{129,128},{128,129},{3,2},{2,3},{131,130},{130,131},{5... | collective-permute-start | bytes 1376264 | tf_op jit(solution)/shard_map/ppermute | solution.py:46
  65.9 3.4 %copy-start.5 = (bf16[128,3584]{1,0:T(8,128)(2,1)}, bf16[128,3584]{1,0:T(8,128)(2,1)S(1)}, u32[]{:S(2)}) copy-start(bf16[128,3584]{1,0:T(8,128)(2,1)S(1)} %collective-permute-done.10.refs_10_) | copy-start | bytes 2752516
  65.9 3.4 %collective-permute-start.15 = (bf16[64,3584]{1,0:T(8,128)(2,1)S(1)}, bf16[64,3584]{1,0:T(8,128)(2,1)S(1)}, u32[]{:S(2)}, u32[]{:S(2)}) collective-permute-start(bf16[64,3584]{1,0:T(8,128)(2,1)S(1)} %collective-permute-done.7.refs_7_), channel_id=1, source_target_pairs={{1,0},{0,1},{129,128},{128,129},{3,2},{2,3},{131,130},{130,131},{5... | collective-permute-start | bytes 1376264 | tf_op jit(solution)/shard_map/ppermute | solution.py:46
  66.4 2.9 %copy-start.6 = (bf16[128,3584]{1,0:T(8,128)(2,1)}, bf16[128,3584]{1,0:T(8,128)(2,1)S(1)}, u32[]{:S(2)}) copy-start(bf16[128,3584]{1,0:T(8,128)(2,1)S(1)} %collective-permute-done.11.refs_11_) | copy-start | bytes 2752516
  66.4 2.9 %copy-start.7 = (bf16[128,3584]{1,0:T(8,128)(2,1)}, bf16[128,3584]{1,0:T(8,128)(2,1)S(1)}, u32[]{:S(2)}) copy-start(bf16[128,3584]{1,0:T(8,128)(2,1)S(1)} %collective-permute-done.12.refs_12_) | copy-start | bytes 2752516
  96.4 16.9 %all-to-all-start.2 = ((f32[32,3,128]{2,1,0:T(4,128)}), f32[32,3,128]{2,1,0:T(4,128)S(1)}, u32[]{:S(2)}, u32[]{:S(2)}) async-start(f32[32,3,128]{2,1,0:T(4,128)} %merge.1), calls=%async_computation.2 | async-start | bytes 131072 | tf_op jit(solution)/shard_map/all_to_all | solution.py:355

commit v3 on v2

--- a/solution.py
+++ b/solution.py
@@ -56,8 +56,7 @@
     ((1, SIDE, FIRST, OWN), (1, SIDE, FIRST, OTHER)),
     ((0, ACROSS, FIRST, OWN), (1, SIDE, SECOND, OWN)),
     ((0, ACROSS, SECOND, OWN), (1, SIDE, SECOND, OTHER)),
-    ((1, ACROSS, FIRST, OWN),),
-    ((1, ACROSS, SECOND, OWN),),
+    ((1, ACROSS, SECOND, OWN), (1, ACROSS, FIRST, OWN)),
 )
 
 
@@ -92,7 +91,7 @@
         each.wait()
 
 
-LATE = (False, False, False, False, False, True, True, True)
+LATE = (False, False, False, False, False, True, True)
 
 
 def arrange_kernel(place, now_ref, next_ref, x_ref, z_ref, sem):
@@ -157,23 +156,27 @@
 
 
 def second_round_kernel(x1_ref, z1_ref, x_ref, sem):
-    copy_rows(((x1_ref, 0, x_ref, 0), (z1_ref, HALF, x_ref, HALF)), sem)
-
-
-def third_round_kernel(x2_ref, z2_ref, x_ref, y_ref, z_ref, sem):
-    copy_rows(
-        ((x2_ref, HALF, x_ref, 0), (x2_ref, 0, y_ref, 0), (z2_ref, HALF, y_ref, HALF), (x2_ref, 0, z_ref, 0)), sem
-    )
-
-
-def rearranged(kernel, values, rows):
+    load = pltpu.make_async_copy(z1_ref.at[pl.ds(HALF, HALF)], x_ref.at[pl.ds(HALF, HALF)], sem)
+    load.start()
+    x_ref[:HALF] = x1_ref[:HALF]
+    load.wait()
+
+
+def third_round_kernel(x2_ref, z2_ref, x_ref, y_ref):
+    x_ref[:HALF] = x2_ref[HALF:]
+    x_ref[HALF:] = z2_ref[:HALF]
+    y_ref[:HALF] = x2_ref[:HALF]
+    y_ref[HALF:] = z2_ref[HALF:]
+
+
+def rearranged(kernel, values, outputs, in_specs, scratch=()):
     return pl.pallas_call(
         kernel,
-        out_shape=tuple(pltpu.VMEM((n, values[0].shape[1]), BF16) for n in rows),
-        in_specs=[ANY] * len(values),
-        out_specs=(VMEM,) * len(rows),
-        scratch_shapes=[pltpu.SemaphoreType.DMA((sum(rows) // CHUNK,))],
-        compiler_params=pltpu.CompilerParams(vmem_limit_bytes=2 * MIB),
+        out_shape=(pltpu.VMEM(values[0].shape, BF16),) * outputs,
+        in_specs=in_specs,
+        out_specs=(VMEM,) * outputs,
+        scratch_shapes=scratch,
+        compiler_params=pltpu.CompilerParams(vmem_limit_bytes=4 * MIB),
         name="rearranged",
     )(*values)
 
@@ -184,12 +187,14 @@
     cot, _, _ = lax.optimization_barrier((cot, x1, z1))
     cot = lax.all_to_all(cot, "dp", 0, 0)
     y2, z2 = receive(x1, "y"), receive(x1, "z")
-    (to_x,) = rearranged(second_round_kernel, (x1, z1), (TOK,))
+    (to_x,) = rearranged(
+        second_round_kernel, (pinned(x1), z1), 1, [VMEM, ANY], [pltpu.SemaphoreType.DMA(())]
+    )
     x2 = receive(to_x, "x")
     y2, z2, x2, cot = lax.optimization_barrier((y2, z2, x2, cot))
-    to_x, to_y, to_z = rearranged(third_round_kernel, (x2, z2), (HALF, TOK, HALF))
-    y3, z3, x3 = receive(to_y, "y"), receive(to_z, "z"), receive(to_x, "x")
-    mine = [x1, z1, y2, z2, x2, y3, z3, x3]
+    to_x, to_y = rearranged(third_round_kernel, (pinned(x2), pinned(z2)), 2, [VMEM, VMEM])
+    y3, x3 = receive(to_y, "y"), receive(to_x, "x")
+    mine = [x1, z1, y2, z2, x2, y3, x3]
     return mine, [swap(v) for v in mine], cot
 
 

time: 114 us -> 112 us (0.982)
  Pallas kernels: 20.8 us -> 17.7 us
  waiting for transfers between devices: 36.3 us -> 38.2 us
  starting transfers between devices: 39.8 us -> 38.5 us
    pallas_call x2, Pallas kernels: 4.21 us -> 1.15 us  [rearranged(): pl.pallas_call(kernel, out_shape=(pltpu.VMEM(values[0].shape, BF16),) * o...]
    ppermute x16 -> x14, waiting for transfers between devices: 27.6 us -> 29.5 us  [receive(): return lax.ppermute(value, ('dp', 'vocab'), pairs)]
    ppermute x16 -> x14, starting transfers between devices: 28.9 us -> 27.6 us  [receive(): return lax.ppermute(value, ('dp', 'vocab'), pairs)]
  transfers between devices with their start and end apart: 18 -> 16, of which waited for: 9 -> 8; matrix products, arithmetic and copies ran while one was open for 0% -> 0% of each run, Pallas kernels for 6% -> 3%
where the time goes in v3:
time: 112 us; the launch traced here: 111 us
  starting transfers between devices  38.5 us (34%)
  waiting for transfers between devices  38.2 us (34%)
  Pallas kernels  17.7 us (16%)
  blocking collectives  15.4 us (14%)
    ppermute x14, waiting for transfers between devices, receive(): return lax.ppermute(value, ('dp', 'vocab'), pairs)  29.5 us
    ppermute x14, starting transfers between devices, receive(): return lax.ppermute(value, ('dp', 'vocab'), pairs)  27.6 us
    all_to_all x1, blocking collectives, shards(): parts = lax.all_to_all(parts, 'dp', 0, 0)  15.4 us
    pallas_call x1, Pallas kernels, update_and_logits(): pl.pallas_call(update_kernel, out_shape=jax.ShapeDtypeStruct(whole, BF16)...  11 us
    all_to_all x1, waiting for transfers between devices, shards(): stat = lax.all_to_all(merge(parts), 'vocab', 0, 0)  8.69 us
    all_to_all x1, starting transfers between devices, shards(): stat = lax.all_to_all(merge(parts), 'vocab', 0, 0)  7.18 us
    all_to_all x1, starting transfers between devices, gather(): cot = lax.all_to_all(cot, 'dp', 0, 0)  3.73 us
  transfers between devices with their start and end apart: 16, of which 8 were waited for; matrix products, arithmetic and copies ran while one was open for 0% of the time, Pallas kernels for 3%

profile of v3, /device:TPU:1, one launch (start us, length us, event | category | flops | bytes accessed | tf_op | source)
XLA Modules:
  0.0 111.4 jit_solution(13620749445275806866)
XLA Ops:
  0.7 0.1 pad_add_fusion.place
  0.8 2.2 %arrange.1 = (bf16[128,3584]{1,0:T(8,128)(2,1)S(1)}, bf16[128,3584]{1,0:T(8,128)(2,1)S(1)}) custom-call(s32[4]{0:T(128)S(1)} %pad_add_fusion.place, bf16[128,3584]{1,0:T(8,128)(2,1)} %now_ref.3, bf16[128,3584]{1,0:T(8,128)(2,1)} %next_ref.3), custom_call_target="tpu_custom_call" | custom-call | tf_op jit(solution)/shard_map/arrange/pallas_call | solution.py:122
  3.0 2.1 %collective-permute-start = (bf16[128,3584]{1,0:T(8,128)(2,1)S(1)}, bf16[128,3584]{1,0:T(8,128)(2,1)S(1)}, u32[]{:S(2)}, u32[]{:S(2)}) collective-permute-start(bf16[128,3584]{1,0:T(8,128)(2,1)S(1)} %get-tuple-element.11), channel_id=1, source_target_pairs={{32,0},{97,1},{160,128},{225,129},{34,2},{99,3},{162,130},{227,131... | collective-permute-start | bytes 2752520 | tf_op jit(solution)/shard_map/ppermute | solution.py:46
  5.1 1.6 %collective-permute-start.1 = (bf16[128,3584]{1,0:T(8,128)(2,1)S(1)}, bf16[128,3584]{1,0:T(8,128)(2,1)}, u32[]{:S(2)}, u32[]{:S(2)}) collective-permute-start(bf16[128,3584]{1,0:T(8,128)(2,1)S(1)} %get-tuple-element.12), channel_id=1, source_target_pairs={{128,0},{135,1},{2,128},{1,129},{130,2},{129,3},{4,130},{3,131},{1... | collective-permute-start | bytes 2752520 | tf_op jit(solution)/shard_map/ppermute | solution.py:46
  6.7 0.7 copy-done.4
  7.4 1.1 prepare.1
  8.5 8.7 %collective-permute-done.x1_ref.refs_0_ = bf16[128,3584]{1,0:T(8,128)(2,1)S(1)} collective-permute-done((bf16[128,3584]{1,0:T(8,128)(2,1)S(1)}, bf16[128,3584]{1,0:T(8,128)(2,1)S(1)}, u32[]{:S(2)}, u32[]{:S(2)}) %collective-permute-start) | collective-permute-done | bytes 917536 | tf_op jit(solution)/shard_map/ppermute | solution.py:46
  17.1 4.4 %collective-permute-done.1.z1_ref.refs_1_ = bf16[128,3584]{1,0:T(8,128)(2,1)} collective-permute-done((bf16[128,3584]{1,0:T(8,128)(2,1)S(1)}, bf16[128,3584]{1,0:T(8,128)(2,1)}, u32[]{:S(2)}, u32[]{:S(2)}) %collective-permute-start.1) | collective-permute-done | bytes 917536 | tf_op jit(solution)/shard_map/ppermute | solution.py:46
  21.6 3.7 %all-to-all-start = ((bf16[8,336,128]{2,1,0:T(8,128)(2,1)}), bf16[8,336,128]{2,1,0:T(8,128)(2,1)S(1)}, u32[]{:S(2)}, u32[]{:S(2)}) async-start(bf16[8,336,128]{2,1,0:T(8,128)(2,1)} %prepare.1), calls=%async_computation | async-start | bytes 1376256 | tf_op jit(solution)/shard_map/all_to_all | solution.py:188
  25.3 1.5 %collective-permute-start.3 = (bf16[128,3584]{1,0:T(8,128)(2,1)S(1)}, bf16[128,3584]{1,0:T(8,128)(2,1)S(1)}, u32[]{:S(2)}, u32[]{:S(2)}) collective-permute-start(bf16[128,3584]{1,0:T(8,128)(2,1)S(1)} %collective-permute-done.x1_ref.refs_0_), channel_id=1, source_target_pairs={{128,0},{135,1},{2,128},{1,129},{130,2},{129,3},{4,130},{3,131},{1... | collective-permute-start | bytes 2752520 | tf_op jit(solution)/shard_map/ppermute | solution.py:46
  26.7 1.3 %collective-permute-start.2 = (bf16[128,3584]{1,0:T(8,128)(2,1)S(1)}, bf16[128,3584]{1,0:T(8,128)(2,1)}, u32[]{:S(2)}, u32[]{:S(2)}) collective-permute-start(bf16[128,3584]{1,0:T(8,128)(2,1)S(1)} %collective-permute-done.x1_ref.refs_0_), channel_id=1, source_target_pairs={{8,0},{25,1},{136,128},{153,129},{10,2},{27,3},{138,130},{155,131}... | collective-permute-start | bytes 2752520 | tf_op jit(solution)/shard_map/ppermute | solution.py:46
  28.1 1.0 rearranged.2
  29.1 1.3 %collective-permute-start.4 = (bf16[128,3584]{1,0:T(8,128)(2,1)S(1)}, bf16[128,3584]{1,0:T(8,128)(2,1)S(1)}, u32[]{:S(2)}, u32[]{:S(2)}) collective-permute-start(bf16[128,3584]{1,0:T(8,128)(2,1)S(1)} %rearranged.2), channel_id=1, source_target_pairs={{32,0},{97,1},{160,128},{225,129},{34,2},{99,3},{162,130},{227,131... | collective-permute-start | bytes 2752520 | tf_op jit(solution)/shard_map/ppermute | solution.py:46
  30.4 7.9 %collective-permute-start.7 = (bf16[128,3584]{1,0:T(8,128)(2,1)S(1)}, bf16[128,3584]{1,0:T(8,128)(2,1)}, u32[]{:S(2)}, u32[]{:S(2)}) collective-permute-start(bf16[128,3584]{1,0:T(8,128)(2,1)S(1)} %collective-permute-done.x1_ref.refs_0_), channel_id=1, source_target_pairs={{1,0},{0,1},{129,128},{128,129},{3,2},{2,3},{131,130},{130,131},{5... | collective-permute-start | bytes 2752520 | tf_op jit(solution)/shard_map/ppermute | solution.py:46
  38.3 5.0 %collective-permute-done.3.z2_ref.refs_3_ = bf16[128,3584]{1,0:T(8,128)(2,1)S(1)} collective-permute-done((bf16[128,3584]{1,0:T(8,128)(2,1)S(1)}, bf16[128,3584]{1,0:T(8,128)(2,1)S(1)}, u32[]{:S(2)}, u32[]{:S(2)}) %collective-permute-start.3) | collective-permute-done | bytes 917536 | tf_op jit(solution)/shard_map/ppermute | solution.py:46
  43.3 3.4 %collective-permute-done.4.x2_ref.refs_4_ = bf16[128,3584]{1,0:T(8,128)(2,1)S(1)} collective-permute-done((bf16[128,3584]{1,0:T(8,128)(2,1)S(1)}, bf16[128,3584]{1,0:T(8,128)(2,1)S(1)}, u32[]{:S(2)}, u32[]{:S(2)}) %collective-permute-start.4) | collective-permute-done | bytes 917536 | tf_op jit(solution)/shard_map/ppermute | solution.py:46
  46.6 0.1 rearranged.3
  46.7 1.4 %collective-permute-start.5 = (bf16[128,3584]{1,0:T(8,128)(2,1)S(1)}, bf16[128,3584]{1,0:T(8,128)(2,1)S(1)}, u32[]{:S(2)}, u32[]{:S(2)}) collective-permute-start(bf16[128,3584]{1,0:T(8,128)(2,1)S(1)} %get-tuple-element.17), channel_id=1, source_target_pairs={{8,0},{25,1},{136,128},{153,129},{10,2},{27,3},{138,130},{155,131}... | collective-permute-start | bytes 2752520 | tf_op jit(solution)/shard_map/ppermute | solution.py:46
  48.2 5.6 %collective-permute-start.10 = (bf16[128,3584]{1,0:T(8,128)(2,1)S(1)}, bf16[128,3584]{1,0:T(8,128)(2,1)S(1)}, u32[]{:S(2)}, u32[]{:S(2)}) collective-permute-start(bf16[128,3584]{1,0:T(8,128)(2,1)S(1)} %collective-permute-done.3.z2_ref.refs_3_), channel_id=1, source_target_pairs={{1,0},{0,1},{129,128},{128,129},{3,2},{2,3},{131,130},{130,131},{5... | collective-permute-start | bytes 2752520 | tf_op jit(solution)/shard_map/ppermute | solution.py:46
  53.8 0.5 collective-permute-start.9
  54.3 6.1 %collective-permute-done.5.refs_5_ = bf16[128,3584]{1,0:T(8,128)(2,1)S(1)} collective-permute-done((bf16[128,3584]{1,0:T(8,128)(2,1)S(1)}, bf16[128,3584]{1,0:T(8,128)(2,1)S(1)}, u32[]{:S(2)}, u32[]{:S(2)}) %collective-permute-start.5) | collective-permute-done | bytes 917536 | tf_op jit(solution)/shard_map/ppermute | solution.py:46
  60.4 2.4 %collective-permute-start.12 = (bf16[128,3584]{1,0:T(8,128)(2,1)S(1)}, bf16[128,3584]{1,0:T(8,128)(2,1)S(1)}, u32[]{:S(2)}, u32[]{:S(2)}) collective-permute-start(bf16[128,3584]{1,0:T(8,128)(2,1)S(1)} %collective-permute-done.5.refs_5_), channel_id=1, source_target_pairs={{1,0},{0,1},{129,128},{128,129},{3,2},{2,3},{131,130},{130,131},{5... | collective-permute-start | bytes 2752520 | tf_op jit(solution)/shard_map/ppermute | solution.py:46
  62.8 1.9 %collective-permute-start.13 = (bf16[128,3584]{1,0:T(8,128)(2,1)S(1)}, bf16[128,3584]{1,0:T(8,128)(2,1)S(1)}, u32[]{:S(2)}, u32[]{:S(2)}) collective-permute-start(bf16[128,3584]{1,0:T(8,128)(2,1)S(1)} %collective-permute-done.6.refs_6_), channel_id=1, source_target_pairs={{1,0},{0,1},{129,128},{128,129},{3,2},{2,3},{131,130},{130,131},{5... | collective-permute-start | bytes 2752520 | tf_op jit(solution)/shard_map/ppermute | solution.py:46
  64.8 0.1 collective-permute-done.12.refs_12_
  64.9 1.9 %collective-permute-done.13.refs_13_ = bf16[128,3584]{1,0:T(8,128)(2,1)S(1)} collective-permute-done((bf16[128,3584]{1,0:T(8,128)(2,1)S(1)}, bf16[128,3584]{1,0:T(8,128)(2,1)S(1)}, u32[]{:S(2)}, u32[]{:S(2)}) %collective-permute-start.13) | collective-permute-done | bytes 917536 | tf_op jit(solution)/shard_map/ppermute | solution.py:46
  66.9 11.0 %update_and_logits.1 = bf16[8,336,128]{2,1,0:T(8,128)(2,1)S(1)} custom-call(s32[4]{0:T(128)S(1)} %pad_add_fusion.place, bf16[128,3584]{1,0:T(8,128)(2,1)} %now_ref.3, bf16[128,3584]{1,0:T(8,128)(2,1)} %next_ref.3, bf16[128,3584]{1,0:T(8,128)(2,1)} %copy-done.2, bf16[128,3584]{1,0:T(8,128)(2,1)} %collective-permute-done.1.z1_ref.refs_1_, ...), custom_call_target="tpu_custom_call" | custom-call | flops 9400000512 | bytes 24000000 | tf_op jit(solution)/shard_map/update_and_logits/pallas_call | solution.py:273
  77.9 15.4 %all_to_all.15.part_ref = bf16[8,336,128]{2,1,0:T(8,128)(2,1)S(1)} all-to-all(bf16[8,336,128]{2,1,0:T(8,128)(2,1)S(1)} %update_and_logits.1), channel_id=1, replica_groups=mesh['dp'=8,'vocab'=32] {'dp'}, dimensions={0} | all-to-all | bytes 1376256 | tf_op jit(solution)/shard_map/all_to_all | solution.py:359
  93.3 0.7 merge.1
  94.0 7.2 %all-to-all-start.2 = ((f32[32,3,128]{2,1,0:T(4,128)}), f32[32,3,128]{2,1,0:T(4,128)S(1)}, u32[]{:S(2)}, u32[]{:S(2)}) async-start(f32[32,3,128]{2,1,0:T(4,128)} %merge.1), calls=%async_computation.2 | async-start | bytes 131072 | tf_op jit(solution)/shard_map/all_to_all | solution.py:360
  101.1 1.1 turn.1
  102.2 8.7 %all-to-all-done.2.stat_ref = f32[32,3,128]{2,1,0:T(4,128)S(1)} async-done(((f32[32,3,128]{2,1,0:T(4,128)}), f32[32,3,128]{2,1,0:T(4,128)S(1)}, u32[]{:S(2)}, u32[]{:S(2)}) %all-to-all-start.2) | async-done | bytes 49184 | tf_op jit(solution)/shard_map/all_to_all | solution.py:360
  110.9 0.6 loss.1
  (26 shorter events, 0.1 us)
Async XLA Ops:
  0.6 6.1 %copy-start.3 = (bf16[128,2560]{1,0:T(8,128)(2,1)S(1)}, bf16[128,2560]{1,0:T(8,128)(2,1)}, u32[]{:S(2)}) copy-start(bf16[128,2560]{1,0:T(8,128)(2,1)} %cot_ref.1) | copy-start | bytes 1966084
  3.0 14.2 %collective-permute-start = (bf16[128,3584]{1,0:T(8,128)(2,1)S(1)}, bf16[128,3584]{1,0:T(8,128)(2,1)S(1)}, u32[]{:S(2)}, u32[]{:S(2)}) collective-permute-start(bf16[128,3584]{1,0:T(8,128)(2,1)S(1)} %get-tuple-element.11), channel_id=1, source_target_pairs={{32,0},{97,1},{160,128},{225,129},{34,2},{99,3},{162,130},{227,131... | collective-permute-start | bytes 2752520 | tf_op jit(solution)/shard_map/ppermute | solution.py:46
  5.1 16.5 %collective-permute-start.1 = (bf16[128,3584]{1,0:T(8,128)(2,1)S(1)}, bf16[128,3584]{1,0:T(8,128)(2,1)}, u32[]{:S(2)}, u32[]{:S(2)}) collective-permute-start(bf16[128,3584]{1,0:T(8,128)(2,1)S(1)} %get-tuple-element.12), channel_id=1, source_target_pairs={{128,0},{135,1},{2,128},{1,129},{130,2},{129,3},{4,130},{3,131},{1... | collective-permute-start | bytes 2752520 | tf_op jit(solution)/shard_map/ppermute | solution.py:46
  6.7 0.7 copy-start.4
  17.1 29.6 %copy-start.2 = (bf16[128,3584]{1,0:T(8,128)(2,1)}, bf16[128,3584]{1,0:T(8,128)(2,1)S(1)}, u32[]{:S(2)}) copy-start(bf16[128,3584]{1,0:T(8,128)(2,1)S(1)} %collective-permute-done.x1_ref.refs_0_) | copy-start | bytes 2752516
  21.6 25.1 %all-to-all-start = ((bf16[8,336,128]{2,1,0:T(8,128)(2,1)}), bf16[8,336,128]{2,1,0:T(8,128)(2,1)S(1)}, u32[]{:S(2)}, u32[]{:S(2)}) async-start(bf16[8,336,128]{2,1,0:T(8,128)(2,1)} %prepare.1), calls=%async_computation | async-start | bytes 1376256 | tf_op jit(solution)/shard_map/all_to_all | solution.py:188
  25.3 18.0 %collective-permute-start.3 = (bf16[128,3584]{1,0:T(8,128)(2,1)S(1)}, bf16[128,3584]{1,0:T(8,128)(2,1)S(1)}, u32[]{:S(2)}, u32[]{:S(2)}) collective-permute-start(bf16[128,3584]{1,0:T(8,128)(2,1)S(1)} %collective-permute-done.x1_ref.refs_0_), channel_id=1, source_target_pairs={{128,0},{135,1},{2,128},{1,129},{130,2},{129,3},{4,130},{3,131},{1... | collective-permute-start | bytes 2752520 | tf_op jit(solution)/shard_map/ppermute | solution.py:46
  26.7 16.5 %collective-permute-start.2 = (bf16[128,3584]{1,0:T(8,128)(2,1)S(1)}, bf16[128,3584]{1,0:T(8,128)(2,1)}, u32[]{:S(2)}, u32[]{:S(2)}) collective-permute-start(bf16[128,3584]{1,0:T(8,128)(2,1)S(1)} %collective-permute-done.x1_ref.refs_0_), channel_id=1, source_target_pairs={{8,0},{25,1},{136,128},{153,129},{10,2},{27,3},{138,130},{155,131}... | collective-permute-start | bytes 2752520 | tf_op jit(solution)/shard_map/ppermute | solution.py:46
  29.1 17.5 %collective-permute-start.4 = (bf16[128,3584]{1,0:T(8,128)(2,1)S(1)}, bf16[128,3584]{1,0:T(8,128)(2,1)S(1)}, u32[]{:S(2)}, u32[]{:S(2)}) collective-permute-start(bf16[128,3584]{1,0:T(8,128)(2,1)S(1)} %rearranged.2), channel_id=1, source_target_pairs={{32,0},{97,1},{160,128},{225,129},{34,2},{99,3},{162,130},{227,131... | collective-permute-start | bytes 2752520 | tf_op jit(solution)/shard_map/ppermute | solution.py:46
  30.4 23.4 %collective-permute-start.7 = (bf16[128,3584]{1,0:T(8,128)(2,1)S(1)}, bf16[128,3584]{1,0:T(8,128)(2,1)}, u32[]{:S(2)}, u32[]{:S(2)}) collective-permute-start(bf16[128,3584]{1,0:T(8,128)(2,1)S(1)} %collective-permute-done.x1_ref.refs_0_), channel_id=1, source_target_pairs={{1,0},{0,1},{129,128},{128,129},{3,2},{2,3},{131,130},{130,131},{5... | collective-permute-start | bytes 2752520 | tf_op jit(solution)/shard_map/ppermute | solution.py:46
  38.3 15.5 %collective-permute-start.8 = (bf16[128,3584]{1,0:T(8,128)(2,1)}, bf16[128,3584]{1,0:T(8,128)(2,1)}, u32[]{:S(2)}, u32[]{:S(2)}) collective-permute-start(bf16[128,3584]{1,0:T(8,128)(2,1)} %collective-permute-done.1.z1_ref.refs_1_), channel_id=1, source_target_pairs={{1,0},{0,1},{129,128},{128,129},{3,2},{2,3},{131,130},{130,131},{5... | collective-permute-start | bytes 2752520 | tf_op jit(solution)/shard_map/ppermute | solution.py:46
  43.2 23.6 %copy-start = (bf16[128,3584]{1,0:T(8,128)(2,1)}, bf16[128,3584]{1,0:T(8,128)(2,1)S(1)}, u32[]{:S(2)}) copy-start(bf16[128,3584]{1,0:T(8,128)(2,1)S(1)} %collective-permute-done.3.z2_ref.refs_3_) | copy-start | bytes 2752516
  46.6 20.2 %copy-start.1 = (bf16[128,3584]{1,0:T(8,128)(2,1)}, bf16[128,3584]{1,0:T(8,128)(2,1)S(1)}, u32[]{:S(2)}) copy-start(bf16[128,3584]{1,0:T(8,128)(2,1)S(1)} %collective-permute-done.4.x2_ref.refs_4_) | copy-start | bytes 2752516
  46.7 13.6 %collective-permute-start.5 = (bf16[128,3584]{1,0:T(8,128)(2,1)S(1)}, bf16[128,3584]{1,0:T(8,128)(2,1)S(1)}, u32[]{:S(2)}, u32[]{:S(2)}) collective-permute-start(bf16[128,3584]{1,0:T(8,128)(2,1)S(1)} %get-tuple-element.17), channel_id=1, source_target_pairs={{8,0},{25,1},{136,128},{153,129},{10,2},{27,3},{138,130},{155,131}... | collective-permute-start | bytes 2752520 | tf_op jit(solution)/shard_map/ppermute | solution.py:46
  48.2 14.7 %collective-permute-start.6 = (bf16[128,3584]{1,0:T(8,128)(2,1)S(1)}, bf16[128,3584]{1,0:T(8,128)(2,1)S(1)}, u32[]{:S(2)}, u32[]{:S(2)}) collective-permute-start(bf16[128,3584]{1,0:T(8,128)(2,1)S(1)} %get-tuple-element.18), channel_id=1, source_target_pairs={{32,0},{97,1},{160,128},{225,129},{34,2},{99,3},{162,130},{227,131... | collective-permute-start | bytes 2752520 | tf_op jit(solution)/shard_map/ppermute | solution.py:46
  48.2 16.6 %collective-permute-start.10 = (bf16[128,3584]{1,0:T(8,128)(2,1)S(1)}, bf16[128,3584]{1,0:T(8,128)(2,1)S(1)}, u32[]{:S(2)}, u32[]{:S(2)}) collective-permute-start(bf16[128,3584]{1,0:T(8,128)(2,1)S(1)} %collective-permute-done.3.z2_ref.refs_3_), channel_id=1, source_target_pairs={{1,0},{0,1},{129,128},{128,129},{3,2},{2,3},{131,130},{130,131},{5... | collective-permute-start | bytes 2752520 | tf_op jit(solution)/shard_map/ppermute | solution.py:46
  53.8 10.9 %collective-permute-start.11 = (bf16[128,3584]{1,0:T(8,128)(2,1)S(1)}, bf16[128,3584]{1,0:T(8,128)(2,1)S(1)}, u32[]{:S(2)}, u32[]{:S(2)}) collective-permute-start(bf16[128,3584]{1,0:T(8,128)(2,1)S(1)} %collective-permute-done.4.x2_ref.refs_4_), channel_id=1, source_target_pairs={{1,0},{0,1},{129,128},{128,129},{3,2},{2,3},{131,130},{130,131},{5... | collective-permute-start | bytes 2752520 | tf_op jit(solution)/shard_map/ppermute | solution.py:46
  53.8 10.9 %collective-permute-start.9 = (bf16[128,3584]{1,0:T(8,128)(2,1)}, bf16[128,3584]{1,0:T(8,128)(2,1)S(1)}, u32[]{:S(2)}, u32[]{:S(2)}) collective-permute-start(bf16[128,3584]{1,0:T(8,128)(2,1)} %collective-permute-done.2.refs_2_), channel_id=1, source_target_pairs={{1,0},{0,1},{129,128},{128,129},{3,2},{2,3},{131,130},{130,131},{5... | collective-permute-start | bytes 2752520 | tf_op jit(solution)/shard_map/ppermute | solution.py:46
  60.4 4.5 %collective-permute-start.12 = (bf16[128,3584]{1,0:T(8,128)(2,1)S(1)}, bf16[128,3584]{1,0:T(8,128)(2,1)S(1)}, u32[]{:S(2)}, u32[]{:S(2)}) collective-permute-start(bf16[128,3584]{1,0:T(8,128)(2,1)S(1)} %collective-permute-done.5.refs_5_), channel_id=1, source_target_pairs={{1,0},{0,1},{129,128},{128,129},{3,2},{2,3},{131,130},{130,131},{5... | collective-permute-start | bytes 2752520 | tf_op jit(solution)/shard_map/ppermute | solution.py:46
  62.8 4.0 %collective-permute-start.13 = (bf16[128,3584]{1,0:T(8,128)(2,1)S(1)}, bf16[128,3584]{1,0:T(8,128)(2,1)S(1)}, u32[]{:S(2)}, u32[]{:S(2)}) collective-permute-start(bf16[128,3584]{1,0:T(8,128)(2,1)S(1)} %collective-permute-done.6.refs_6_), channel_id=1, source_target_pairs={{1,0},{0,1},{129,128},{128,129},{3,2},{2,3},{131,130},{130,131},{5... | collective-permute-start | bytes 2752520 | tf_op jit(solution)/shard_map/ppermute | solution.py:46
  64.7 2.1 %copy-start.7 = (bf16[128,3584]{1,0:T(8,128)(2,1)}, bf16[128,3584]{1,0:T(8,128)(2,1)S(1)}, u32[]{:S(2)}) copy-start(bf16[128,3584]{1,0:T(8,128)(2,1)S(1)} %collective-permute-done.9.refs_9_) | copy-start | bytes 2752516
  64.7 2.1 %copy-start.5 = (bf16[128,3584]{1,0:T(8,128)(2,1)}, bf16[128,3584]{1,0:T(8,128)(2,1)S(1)}, u32[]{:S(2)}) copy-start(bf16[128,3584]{1,0:T(8,128)(2,1)S(1)} %collective-permute-done.10.refs_10_) | copy-start | bytes 2752516
  64.8 2.1 %copy-start.6 = (bf16[128,3584]{1,0:T(8,128)(2,1)}, bf16[128,3584]{1,0:T(8,128)(2,1)S(1)}, u32[]{:S(2)}) copy-start(bf16[128,3584]{1,0:T(8,128)(2,1)S(1)} %collective-permute-done.11.refs_11_) | copy-start | bytes 2752516
  94.0 16.9 %all-to-all-start.2 = ((f32[32,3,128]{2,1,0:T(4,128)}), f32[32,3,128]{2,1,0:T(4,128)S(1)}, u32[]{:S(2)}, u32[]{:S(2)}) async-start(f32[32,3,128]{2,1,0:T(4,128)} %merge.1), calls=%async_computation.2 | async-start | bytes 131072 | tf_op jit(solution)/shard_map/all_to_all | solution.py:360

commit v4 on v3

--- a/solution.py
+++ b/solution.py
@@ -100,14 +100,9 @@
 
     def copy(first_ref, second_ref):
         copy_rows(
-            (
-                (first_ref, own, x_ref, 0),
-                (first_ref, other, x_ref, HALF),
-                (first_ref, own, z_ref, 0),
-                (second_ref, own, z_ref, HALF),
-            ),
-            sem,
+            ((first_ref, own, x_ref, 0), (second_ref, own, z_ref, HALF), (first_ref, other, x_ref, HALF)), sem
         )
+        z_ref[:HALF] = x_ref[:HALF]
 
     @pl.when(odd == 0)
     def _():
@@ -184,7 +179,7 @@
 def gather(to_x, to_z, cot):
     swap = lambda v: receive(v, "core")
     x1, z1 = receive(to_x, "x"), receive(to_z, "z")
-    cot, _, _ = lax.optimization_barrier((cot, x1, z1))
+    cot, _ = lax.optimization_barrier((cot, x1))
     cot = lax.all_to_all(cot, "dp", 0, 0)
     y2, z2 = receive(x1, "y"), receive(x1, "z")
     (to_x,) = rearranged(
@@ -238,7 +233,9 @@
         master, moment, second = (target[:, columns(step)].astype(F32) for target in kept)
         moment_new = beta_one * moment + (1.0 - beta_one) * gradient
         second_new = beta_two * second + (1.0 - beta_two) * gradient * gradient
-        rows_new = master - learn_rate * (moment_new / (jnp.sqrt(second_new) + epsilon) + decay_rate * master)
+        root = second_new * lax.rsqrt(second_new)
+        scale = lax.rsqrt(second_new + epsilon * (2.0 * root + epsilon))
+        rows_new = (1.0 - learn_rate * decay_rate) * master - learn_rate * (moment_new * scale)
         product = lax.dot_general(
             rows_new.astype(BF16), hidden[1, :, columns(step)], (((1,), (1,)), ((), ())), preferred_element_type=F32
         )

time: 112 us -> 110 us (0.982)
  waiting for transfers between devices: 38.2 us -> 29.3 us
  starting transfers between devices: 38.5 us -> 46 us
    ppermute x14, waiting for transfers between devices: 29.5 us -> 20.6 us  [receive(): return lax.ppermute(value, ('dp', 'vocab'), pairs)]
    ppermute x14, starting transfers between devices: 27.6 us -> 34.6 us  [receive(): return lax.ppermute(value, ('dp', 'vocab'), pairs)]
  transfers between devices with their start and end apart: 16 -> 16, of which waited for: 8 -> 7; matrix products, arithmetic and copies ran while one was open for 0% -> 0% of each run, Pallas kernels for 3% -> 3%
where the time goes in v4:
time: 110 us
  starting transfers between devices  46 us (42%)
  waiting for transfers between devices  29.3 us (27%)
  Pallas kernels  17.2 us (16%)
  blocking collectives  15.4 us (14%)
    ppermute x14, starting transfers between devices, receive(): return lax.ppermute(value, ('dp', 'vocab'), pairs)  34.6 us
    ppermute x14, waiting for transfers between devices, receive(): return lax.ppermute(value, ('dp', 'vocab'), pairs)  20.6 us
    all_to_all x1, blocking collectives, shards(): parts = lax.all_to_all(parts, 'dp', 0, 0)  15.4 us
    pallas_call x1, Pallas kernels, update_and_logits(): pl.pallas_call(update_kernel, out_shape=jax.ShapeDtypeStruct(whole, BF16)...  10.6 us
    all_to_all x1, waiting for transfers between devices, shards(): stat = lax.all_to_all(merge(parts), 'vocab', 0, 0)  8.69 us
    all_to_all x1, starting transfers between devices, shards(): stat = lax.all_to_all(merge(parts), 'vocab', 0, 0)  6.68 us
    all_to_all x1, starting transfers between devices, gather(): cot = lax.all_to_all(cot, 'dp', 0, 0)  4.76 us
  transfers between devices with their start and end apart: 16, of which 7 were waited for; matrix products, arithmetic and copies ran while one was open for 0% of the time, Pallas kernels for 3%

profile of v4, /device:TPU:1, one launch (start us, length us, event | category | flops | bytes accessed | tf_op | source)
XLA Modules:
  0.0 109.5 jit_solution(1190173537309164998)
XLA Ops:
  0.7 0.1 pad_add_fusion.place
  0.8 2.1 %arrange.1 = (bf16[128,3584]{1,0:T(8,128)(2,1)S(1)}, bf16[128,3584]{1,0:T(8,128)(2,1)S(1)}) custom-call(s32[4]{0:T(128)S(1)} %pad_add_fusion.place, bf16[128,3584]{1,0:T(8,128)(2,1)} %now_ref.3, bf16[128,3584]{1,0:T(8,128)(2,1)} %next_ref.3), custom_call_target="tpu_custom_call" | custom-call | tf_op jit(solution)/shard_map/arrange/pallas_call | solution.py:117
  2.9 2.1 %collective-permute-start = (bf16[128,3584]{1,0:T(8,128)(2,1)S(1)}, bf16[128,3584]{1,0:T(8,128)(2,1)S(1)}, u32[]{:S(2)}, u32[]{:S(2)}) collective-permute-start(bf16[128,3584]{1,0:T(8,128)(2,1)S(1)} %get-tuple-element.11), channel_id=1, source_target_pairs={{32,0},{97,1},{160,128},{225,129},{34,2},{99,3},{162,130},{227,131... | collective-permute-start | bytes 2752520 | tf_op jit(solution)/shard_map/ppermute | solution.py:46
  5.0 1.6 %collective-permute-start.1 = (bf16[128,3584]{1,0:T(8,128)(2,1)S(1)}, bf16[128,3584]{1,0:T(8,128)(2,1)}, u32[]{:S(2)}, u32[]{:S(2)}) collective-permute-start(bf16[128,3584]{1,0:T(8,128)(2,1)S(1)} %get-tuple-element.12), channel_id=1, source_target_pairs={{128,0},{135,1},{2,128},{1,129},{130,2},{129,3},{4,130},{3,131},{1... | collective-permute-start | bytes 2752520 | tf_op jit(solution)/shard_map/ppermute | solution.py:46
  6.6 0.7 copy-done.4
  7.3 1.1 prepare.1
  8.4 8.7 %collective-permute-done.x1_ref.refs_0_ = bf16[128,3584]{1,0:T(8,128)(2,1)S(1)} collective-permute-done((bf16[128,3584]{1,0:T(8,128)(2,1)S(1)}, bf16[128,3584]{1,0:T(8,128)(2,1)S(1)}, u32[]{:S(2)}, u32[]{:S(2)}) %collective-permute-start) | collective-permute-done | bytes 917536 | tf_op jit(solution)/shard_map/ppermute | solution.py:46
  17.0 4.8 %all-to-all-start = ((bf16[8,336,128]{2,1,0:T(8,128)(2,1)}), bf16[8,336,128]{2,1,0:T(8,128)(2,1)S(1)}, u32[]{:S(2)}, u32[]{:S(2)}) async-start(bf16[8,336,128]{2,1,0:T(8,128)(2,1)} %prepare.1), calls=%async_computation | async-start | bytes 1376256 | tf_op jit(solution)/shard_map/all_to_all | solution.py:183
  21.8 1.5 %collective-permute-start.3 = (bf16[128,3584]{1,0:T(8,128)(2,1)S(1)}, bf16[128,3584]{1,0:T(8,128)(2,1)S(1)}, u32[]{:S(2)}, u32[]{:S(2)}) collective-permute-start(bf16[128,3584]{1,0:T(8,128)(2,1)S(1)} %collective-permute-done.x1_ref.refs_0_), channel_id=1, source_target_pairs={{128,0},{135,1},{2,128},{1,129},{130,2},{129,3},{4,130},{3,131},{1... | collective-permute-start | bytes 2752520 | tf_op jit(solution)/shard_map/ppermute | solution.py:46
  23.3 1.3 %collective-permute-start.2 = (bf16[128,3584]{1,0:T(8,128)(2,1)S(1)}, bf16[128,3584]{1,0:T(8,128)(2,1)}, u32[]{:S(2)}, u32[]{:S(2)}) collective-permute-start(bf16[128,3584]{1,0:T(8,128)(2,1)S(1)} %collective-permute-done.x1_ref.refs_0_), channel_id=1, source_target_pairs={{8,0},{25,1},{136,128},{153,129},{10,2},{27,3},{138,130},{155,131}... | collective-permute-start | bytes 2752520 | tf_op jit(solution)/shard_map/ppermute | solution.py:46
  24.6 1.0 rearranged.2
  25.6 1.3 %collective-permute-start.4 = (bf16[128,3584]{1,0:T(8,128)(2,1)S(1)}, bf16[128,3584]{1,0:T(8,128)(2,1)S(1)}, u32[]{:S(2)}, u32[]{:S(2)}) collective-permute-start(bf16[128,3584]{1,0:T(8,128)(2,1)S(1)} %rearranged.2), channel_id=1, source_target_pairs={{32,0},{97,1},{160,128},{225,129},{34,2},{99,3},{162,130},{227,131... | collective-permute-start | bytes 2752520 | tf_op jit(solution)/shard_map/ppermute | solution.py:46
  26.9 10.4 %collective-permute-start.7 = (bf16[128,3584]{1,0:T(8,128)(2,1)S(1)}, bf16[128,3584]{1,0:T(8,128)(2,1)}, u32[]{:S(2)}, u32[]{:S(2)}) collective-permute-start(bf16[128,3584]{1,0:T(8,128)(2,1)S(1)} %collective-permute-done.x1_ref.refs_0_), channel_id=1, source_target_pairs={{1,0},{0,1},{129,128},{128,129},{3,2},{2,3},{131,130},{130,131},{5... | collective-permute-start | bytes 2752520 | tf_op jit(solution)/shard_map/ppermute | solution.py:46
  37.2 2.6 %collective-permute-done.3.z2_ref.refs_3_ = bf16[128,3584]{1,0:T(8,128)(2,1)S(1)} collective-permute-done((bf16[128,3584]{1,0:T(8,128)(2,1)S(1)}, bf16[128,3584]{1,0:T(8,128)(2,1)S(1)}, u32[]{:S(2)}, u32[]{:S(2)}) %collective-permute-start.3) | collective-permute-done | bytes 917536 | tf_op jit(solution)/shard_map/ppermute | solution.py:46
  39.8 3.3 %collective-permute-done.4.x2_ref.refs_4_ = bf16[128,3584]{1,0:T(8,128)(2,1)S(1)} collective-permute-done((bf16[128,3584]{1,0:T(8,128)(2,1)S(1)}, bf16[128,3584]{1,0:T(8,128)(2,1)S(1)}, u32[]{:S(2)}, u32[]{:S(2)}) %collective-permute-start.4) | collective-permute-done | bytes 917536 | tf_op jit(solution)/shard_map/ppermute | solution.py:46
  43.1 0.1 rearranged.3
  43.3 1.4 %collective-permute-start.5 = (bf16[128,3584]{1,0:T(8,128)(2,1)S(1)}, bf16[128,3584]{1,0:T(8,128)(2,1)S(1)}, u32[]{:S(2)}, u32[]{:S(2)}) collective-permute-start(bf16[128,3584]{1,0:T(8,128)(2,1)S(1)} %get-tuple-element.17), channel_id=1, source_target_pairs={{8,0},{25,1},{136,128},{153,129},{10,2},{27,3},{138,130},{155,131}... | collective-permute-start | bytes 2752520 | tf_op jit(solution)/shard_map/ppermute | solution.py:46
  44.6 8.1 %collective-permute-start.10 = (bf16[128,3584]{1,0:T(8,128)(2,1)S(1)}, bf16[128,3584]{1,0:T(8,128)(2,1)S(1)}, u32[]{:S(2)}, u32[]{:S(2)}) collective-permute-start(bf16[128,3584]{1,0:T(8,128)(2,1)S(1)} %collective-permute-done.3.z2_ref.refs_3_), channel_id=1, source_target_pairs={{1,0},{0,1},{129,128},{128,129},{3,2},{2,3},{131,130},{130,131},{5... | collective-permute-start | bytes 2752520 | tf_op jit(solution)/shard_map/ppermute | solution.py:46
  52.8 0.0 collective-permute-start.11
  52.8 0.5 collective-permute-start.9
  53.3 4.0 %collective-permute-done.5.refs_5_ = bf16[128,3584]{1,0:T(8,128)(2,1)S(1)} collective-permute-done((bf16[128,3584]{1,0:T(8,128)(2,1)S(1)}, bf16[128,3584]{1,0:T(8,128)(2,1)S(1)}, u32[]{:S(2)}, u32[]{:S(2)}) %collective-permute-start.5) | collective-permute-done | bytes 917536 | tf_op jit(solution)/shard_map/ppermute | solution.py:46
  57.3 4.5 %collective-permute-start.12 = (bf16[128,3584]{1,0:T(8,128)(2,1)S(1)}, bf16[128,3584]{1,0:T(8,128)(2,1)S(1)}, u32[]{:S(2)}, u32[]{:S(2)}) collective-permute-start(bf16[128,3584]{1,0:T(8,128)(2,1)S(1)} %collective-permute-done.5.refs_5_), channel_id=1, source_target_pairs={{1,0},{0,1},{129,128},{128,129},{3,2},{2,3},{131,130},{130,131},{5... | collective-permute-start | bytes 2752520 | tf_op jit(solution)/shard_map/ppermute | solution.py:46
  61.7 1.9 %collective-permute-start.13 = (bf16[128,3584]{1,0:T(8,128)(2,1)S(1)}, bf16[128,3584]{1,0:T(8,128)(2,1)S(1)}, u32[]{:S(2)}, u32[]{:S(2)}) collective-permute-start(bf16[128,3584]{1,0:T(8,128)(2,1)S(1)} %collective-permute-done.6.refs_6_), channel_id=1, source_target_pairs={{1,0},{0,1},{129,128},{128,129},{3,2},{2,3},{131,130},{130,131},{5... | collective-permute-start | bytes 2752520 | tf_op jit(solution)/shard_map/ppermute | solution.py:46
  63.7 0.1 collective-permute-done.12.refs_12_
  63.8 2.0 %collective-permute-done.13.refs_13_ = bf16[128,3584]{1,0:T(8,128)(2,1)S(1)} collective-permute-done((bf16[128,3584]{1,0:T(8,128)(2,1)S(1)}, bf16[128,3584]{1,0:T(8,128)(2,1)S(1)}, u32[]{:S(2)}, u32[]{:S(2)}) %collective-permute-start.13) | collective-permute-done | bytes 917536 | tf_op jit(solution)/shard_map/ppermute | solution.py:46
  65.8 10.6 %update_and_logits.1 = bf16[8,336,128]{2,1,0:T(8,128)(2,1)S(1)} custom-call(s32[4]{0:T(128)S(1)} %pad_add_fusion.place, bf16[128,3584]{1,0:T(8,128)(2,1)} %now_ref.3, bf16[128,3584]{1,0:T(8,128)(2,1)} %next_ref.3, bf16[128,3584]{1,0:T(8,128)(2,1)} %copy-done.2, bf16[128,3584]{1,0:T(8,128)(2,1)} %collective-permute-done.1.z1_ref.refs_1_, ...), custom_call_target="tpu_custom_call" | custom-call | flops 9400000512 | bytes 24000000 | tf_op jit(solution)/shard_map/update_and_logits/pallas_call | solution.py:270
  76.4 15.4 %all_to_all.15.part_ref = bf16[8,336,128]{2,1,0:T(8,128)(2,1)S(1)} all-to-all(bf16[8,336,128]{2,1,0:T(8,128)(2,1)S(1)} %update_and_logits.1), channel_id=1, replica_groups=mesh['dp'=8,'vocab'=32] {'dp'}, dimensions={0} | all-to-all | bytes 1376256 | tf_op jit(solution)/shard_map/all_to_all | solution.py:356
  91.9 0.7 merge.1
  92.5 6.7 %all-to-all-start.2 = ((f32[32,3,128]{2,1,0:T(4,128)}), f32[32,3,128]{2,1,0:T(4,128)S(1)}, u32[]{:S(2)}, u32[]{:S(2)}) async-start(f32[32,3,128]{2,1,0:T(4,128)} %merge.1), calls=%async_computation.2 | async-start | bytes 131072 | tf_op jit(solution)/shard_map/all_to_all | solution.py:357
  99.2 1.1 turn.1
  100.3 8.7 %all-to-all-done.2.stat_ref = f32[32,3,128]{2,1,0:T(4,128)S(1)} async-done(((f32[32,3,128]{2,1,0:T(4,128)}), f32[32,3,128]{2,1,0:T(4,128)S(1)}, u32[]{:S(2)}, u32[]{:S(2)}) %all-to-all-start.2) | async-done | bytes 49184 | tf_op jit(solution)/shard_map/all_to_all | solution.py:357
  109.0 0.6 loss.1
  (26 shorter events, 0.1 us)
Async XLA Ops:
  0.6 6.0 %copy-start.3 = (bf16[128,2560]{1,0:T(8,128)(2,1)S(1)}, bf16[128,2560]{1,0:T(8,128)(2,1)}, u32[]{:S(2)}) copy-start(bf16[128,2560]{1,0:T(8,128)(2,1)} %cot_ref.1) | copy-start | bytes 1966084
  2.9 14.2 %collective-permute-start = (bf16[128,3584]{1,0:T(8,128)(2,1)S(1)}, bf16[128,3584]{1,0:T(8,128)(2,1)S(1)}, u32[]{:S(2)}, u32[]{:S(2)}) collective-permute-start(bf16[128,3584]{1,0:T(8,128)(2,1)S(1)} %get-tuple-element.11), channel_id=1, source_target_pairs={{32,0},{97,1},{160,128},{225,129},{34,2},{99,3},{162,130},{227,131... | collective-permute-start | bytes 2752520 | tf_op jit(solution)/shard_map/ppermute | solution.py:46
  5.0 19.6 %collective-permute-start.1 = (bf16[128,3584]{1,0:T(8,128)(2,1)S(1)}, bf16[128,3584]{1,0:T(8,128)(2,1)}, u32[]{:S(2)}, u32[]{:S(2)}) collective-permute-start(bf16[128,3584]{1,0:T(8,128)(2,1)S(1)} %get-tuple-element.12), channel_id=1, source_target_pairs={{128,0},{135,1},{2,128},{1,129},{130,2},{129,3},{4,130},{3,131},{1... | collective-permute-start | bytes 2752520 | tf_op jit(solution)/shard_map/ppermute | solution.py:46
  6.6 0.7 copy-start.4
  17.0 26.2 %copy-start.2 = (bf16[128,3584]{1,0:T(8,128)(2,1)}, bf16[128,3584]{1,0:T(8,128)(2,1)S(1)}, u32[]{:S(2)}) copy-start(bf16[128,3584]{1,0:T(8,128)(2,1)S(1)} %collective-permute-done.x1_ref.refs_0_) | copy-start | bytes 2752516
  17.0 26.1 %all-to-all-start = ((bf16[8,336,128]{2,1,0:T(8,128)(2,1)}), bf16[8,336,128]{2,1,0:T(8,128)(2,1)S(1)}, u32[]{:S(2)}, u32[]{:S(2)}) async-start(bf16[8,336,128]{2,1,0:T(8,128)(2,1)} %prepare.1), calls=%async_computation | async-start | bytes 1376256 | tf_op jit(solution)/shard_map/all_to_all | solution.py:183
  21.8 18.0 %collective-permute-start.3 = (bf16[128,3584]{1,0:T(8,128)(2,1)S(1)}, bf16[128,3584]{1,0:T(8,128)(2,1)S(1)}, u32[]{:S(2)}, u32[]{:S(2)}) collective-permute-start(bf16[128,3584]{1,0:T(8,128)(2,1)S(1)} %collective-permute-done.x1_ref.refs_0_), channel_id=1, source_target_pairs={{128,0},{135,1},{2,128},{1,129},{130,2},{129,3},{4,130},{3,131},{1... | collective-permute-start | bytes 2752520 | tf_op jit(solution)/shard_map/ppermute | solution.py:46
  23.3 16.5 %collective-permute-start.2 = (bf16[128,3584]{1,0:T(8,128)(2,1)S(1)}, bf16[128,3584]{1,0:T(8,128)(2,1)}, u32[]{:S(2)}, u32[]{:S(2)}) collective-permute-start(bf16[128,3584]{1,0:T(8,128)(2,1)S(1)} %collective-permute-done.x1_ref.refs_0_), channel_id=1, source_target_pairs={{8,0},{25,1},{136,128},{153,129},{10,2},{27,3},{138,130},{155,131}... | collective-permute-start | bytes 2752520 | tf_op jit(solution)/shard_map/ppermute | solution.py:46
  25.6 17.5 %collective-permute-start.4 = (bf16[128,3584]{1,0:T(8,128)(2,1)S(1)}, bf16[128,3584]{1,0:T(8,128)(2,1)S(1)}, u32[]{:S(2)}, u32[]{:S(2)}) collective-permute-start(bf16[128,3584]{1,0:T(8,128)(2,1)S(1)} %rearranged.2), channel_id=1, source_target_pairs={{32,0},{97,1},{160,128},{225,129},{34,2},{99,3},{162,130},{227,131... | collective-permute-start | bytes 2752520 | tf_op jit(solution)/shard_map/ppermute | solution.py:46
  26.9 25.9 %collective-permute-start.7 = (bf16[128,3584]{1,0:T(8,128)(2,1)S(1)}, bf16[128,3584]{1,0:T(8,128)(2,1)}, u32[]{:S(2)}, u32[]{:S(2)}) collective-permute-start(bf16[128,3584]{1,0:T(8,128)(2,1)S(1)} %collective-permute-done.x1_ref.refs_0_), channel_id=1, source_target_pairs={{1,0},{0,1},{129,128},{128,129},{3,2},{2,3},{131,130},{130,131},{5... | collective-permute-start | bytes 2752520 | tf_op jit(solution)/shard_map/ppermute | solution.py:46
  37.2 15.6 %collective-permute-start.8 = (bf16[128,3584]{1,0:T(8,128)(2,1)}, bf16[128,3584]{1,0:T(8,128)(2,1)}, u32[]{:S(2)}, u32[]{:S(2)}) collective-permute-start(bf16[128,3584]{1,0:T(8,128)(2,1)} %collective-permute-done.1.z1_ref.refs_1_), channel_id=1, source_target_pairs={{1,0},{0,1},{129,128},{128,129},{3,2},{2,3},{131,130},{130,131},{5... | collective-permute-start | bytes 2752520 | tf_op jit(solution)/shard_map/ppermute | solution.py:46
  39.8 26.0 %copy-start = (bf16[128,3584]{1,0:T(8,128)(2,1)}, bf16[128,3584]{1,0:T(8,128)(2,1)S(1)}, u32[]{:S(2)}) copy-start(bf16[128,3584]{1,0:T(8,128)(2,1)S(1)} %collective-permute-done.3.z2_ref.refs_3_) | copy-start | bytes 2752516
  43.1 22.7 %copy-start.1 = (bf16[128,3584]{1,0:T(8,128)(2,1)}, bf16[128,3584]{1,0:T(8,128)(2,1)S(1)}, u32[]{:S(2)}) copy-start(bf16[128,3584]{1,0:T(8,128)(2,1)S(1)} %collective-permute-done.4.x2_ref.refs_4_) | copy-start | bytes 2752516
  43.3 14.0 %collective-permute-start.5 = (bf16[128,3584]{1,0:T(8,128)(2,1)S(1)}, bf16[128,3584]{1,0:T(8,128)(2,1)S(1)}, u32[]{:S(2)}, u32[]{:S(2)}) collective-permute-start(bf16[128,3584]{1,0:T(8,128)(2,1)S(1)} %get-tuple-element.17), channel_id=1, source_target_pairs={{8,0},{25,1},{136,128},{153,129},{10,2},{27,3},{138,130},{155,131}... | collective-permute-start | bytes 2752520 | tf_op jit(solution)/shard_map/ppermute | solution.py:46
  44.6 17.1 %collective-permute-start.6 = (bf16[128,3584]{1,0:T(8,128)(2,1)S(1)}, bf16[128,3584]{1,0:T(8,128)(2,1)S(1)}, u32[]{:S(2)}, u32[]{:S(2)}) collective-permute-start(bf16[128,3584]{1,0:T(8,128)(2,1)S(1)} %get-tuple-element.18), channel_id=1, source_target_pairs={{32,0},{97,1},{160,128},{225,129},{34,2},{99,3},{162,130},{227,131... | collective-permute-start | bytes 2752520 | tf_op jit(solution)/shard_map/ppermute | solution.py:46
  44.6 19.1 %collective-permute-start.10 = (bf16[128,3584]{1,0:T(8,128)(2,1)S(1)}, bf16[128,3584]{1,0:T(8,128)(2,1)S(1)}, u32[]{:S(2)}, u32[]{:S(2)}) collective-permute-start(bf16[128,3584]{1,0:T(8,128)(2,1)S(1)} %collective-permute-done.3.z2_ref.refs_3_), channel_id=1, source_target_pairs={{1,0},{0,1},{129,128},{128,129},{3,2},{2,3},{131,130},{130,131},{5... | collective-permute-start | bytes 2752520 | tf_op jit(solution)/shard_map/ppermute | solution.py:46
  52.8 10.9 %collective-permute-start.11 = (bf16[128,3584]{1,0:T(8,128)(2,1)S(1)}, bf16[128,3584]{1,0:T(8,128)(2,1)S(1)}, u32[]{:S(2)}, u32[]{:S(2)}) collective-permute-start(bf16[128,3584]{1,0:T(8,128)(2,1)S(1)} %collective-permute-done.4.x2_ref.refs_4_), channel_id=1, source_target_pairs={{1,0},{0,1},{129,128},{128,129},{3,2},{2,3},{131,130},{130,131},{5... | collective-permute-start | bytes 2752520 | tf_op jit(solution)/shard_map/ppermute | solution.py:46
  52.8 10.9 %collective-permute-start.9 = (bf16[128,3584]{1,0:T(8,128)(2,1)}, bf16[128,3584]{1,0:T(8,128)(2,1)S(1)}, u32[]{:S(2)}, u32[]{:S(2)}) collective-permute-start(bf16[128,3584]{1,0:T(8,128)(2,1)} %collective-permute-done.2.refs_2_), channel_id=1, source_target_pairs={{1,0},{0,1},{129,128},{128,129},{3,2},{2,3},{131,130},{130,131},{5... | collective-permute-start | bytes 2752520 | tf_op jit(solution)/shard_map/ppermute | solution.py:46
  57.3 6.6 %collective-permute-start.12 = (bf16[128,3584]{1,0:T(8,128)(2,1)S(1)}, bf16[128,3584]{1,0:T(8,128)(2,1)S(1)}, u32[]{:S(2)}, u32[]{:S(2)}) collective-permute-start(bf16[128,3584]{1,0:T(8,128)(2,1)S(1)} %collective-permute-done.5.refs_5_), channel_id=1, source_target_pairs={{1,0},{0,1},{129,128},{128,129},{3,2},{2,3},{131,130},{130,131},{5... | collective-permute-start | bytes 2752520 | tf_op jit(solution)/shard_map/ppermute | solution.py:46
  61.7 4.0 %collective-permute-start.13 = (bf16[128,3584]{1,0:T(8,128)(2,1)S(1)}, bf16[128,3584]{1,0:T(8,128)(2,1)S(1)}, u32[]{:S(2)}, u32[]{:S(2)}) collective-permute-start(bf16[128,3584]{1,0:T(8,128)(2,1)S(1)} %collective-permute-done.6.refs_6_), channel_id=1, source_target_pairs={{1,0},{0,1},{129,128},{128,129},{3,2},{2,3},{131,130},{130,131},{5... | collective-permute-start | bytes 2752520 | tf_op jit(solution)/shard_map/ppermute | solution.py:46
  63.7 2.1 %copy-start.7 = (bf16[128,3584]{1,0:T(8,128)(2,1)}, bf16[128,3584]{1,0:T(8,128)(2,1)S(1)}, u32[]{:S(2)}) copy-start(bf16[128,3584]{1,0:T(8,128)(2,1)S(1)} %collective-permute-done.9.refs_9_) | copy-start | bytes 2752516
  63.7 2.1 %copy-start.5 = (bf16[128,3584]{1,0:T(8,128)(2,1)}, bf16[128,3584]{1,0:T(8,128)(2,1)S(1)}, u32[]{:S(2)}) copy-start(bf16[128,3584]{1,0:T(8,128)(2,1)S(1)} %collective-permute-done.10.refs_10_) | copy-start | bytes 2752516
  63.7 2.1 %copy-start.6 = (bf16[128,3584]{1,0:T(8,128)(2,1)}, bf16[128,3584]{1,0:T(8,128)(2,1)S(1)}, u32[]{:S(2)}) copy-start(bf16[128,3584]{1,0:T(8,128)(2,1)S(1)} %collective-permute-done.11.refs_11_) | copy-start | bytes 2752516
  92.5 16.4 %all-to-all-start.2 = ((f32[32,3,128]{2,1,0:T(4,128)}), f32[32,3,128]{2,1,0:T(4,128)S(1)}, u32[]{:S(2)}, u32[]{:S(2)}) async-start(f32[32,3,128]{2,1,0:T(4,128)} %merge.1), calls=%async_computation.2 | async-start | bytes 131072 | tf_op jit(solution)/shard_map/all_to_all | solution.py:357

commit v5 on v4

--- a/solution.py
+++ b/solution.py
@@ -41,7 +41,7 @@
                         source = device_number(x, y, z, 1 - core)
                     else:
                         dx, dy, dz = (step if axis in axes else 0 for axis in "xyz")
-                        source = device_number((x + dx) % NX, (y + dy) % NY, (z + dz) % NZ, core)
+                        source = device_number((x + dx) % NX, (y + dy) % NY, (z - dz) % NZ, core)
                     pairs.append((source, device_number(x, y, z, core)))
     return lax.ppermute(value, ("dp", "vocab"), pairs)
 
@@ -223,13 +223,17 @@
 
     for g in range(N_DP):
         cot_t[:, g * TOK : (g + 1) * TOK] = cot_ref[g, :ROWS]
+    def gradient_of(step):
+        for ref in (hidden, *kept):
+            now = ref.at[..., columns(step)]
+            pltpu.make_async_copy(now, now, sems.at[step]).wait()
+        return jnp.dot(cot_t[...], hidden[0, :, columns(step)], preferred_element_type=F32)
+
+    following = gradient_of(0)
     for step in range(steps):
-        now = hidden.at[:, :, columns(step)]
-        pltpu.make_async_copy(now, now, sems.at[step]).wait()
-        for target in kept:
-            now = target.at[:, columns(step)]
-            pltpu.make_async_copy(now, now, sems.at[step]).wait()
-        gradient = jnp.dot(cot_t[...], hidden[0, :, columns(step)], preferred_element_type=F32)
+        gradient = following
+        if step + 1 < steps:
+            following = gradient_of(step + 1)
         master, moment, second = (target[:, columns(step)].astype(F32) for target in kept)
         moment_new = beta_one * moment + (1.0 - beta_one) * gradient
         second_new = beta_two * second + (1.0 - beta_two) * gradient * gradient

time: 110 us -> 110 us (level)
  starting transfers between devices: 46 us -> 37.1 us
  waiting for transfers between devices: 29.3 us -> 36.6 us
  blocking collectives: 15.4 us -> 17.2 us
    ppermute x14, starting transfers between devices: 34.6 us -> 23.7 us  [receive(): return lax.ppermute(value, ('dp', 'vocab'), pairs)]
    ppermute x14, waiting for transfers between devices: 20.6 us -> 28 us  [receive(): return lax.ppermute(value, ('dp', 'vocab'), pairs)]
    all_to_all x1, starting transfers between devices: 6.68 us -> 9.01 us  [shards(): stat = lax.all_to_all(merge(parts), 'vocab', 0, 0)]
    all_to_all x1, blocking collectives: 15.4 us -> 17.2 us  [shards(): parts = lax.all_to_all(parts, 'dp', 0, 0)]
  transfers between devices with their start and end apart: 16 -> 16, of which waited for: 7 -> 8; matrix products, arithmetic and copies ran while one was open for 0% -> 0% of each run, Pallas kernels for 3% -> 3%
where the time goes in v5:
time: 110 us; the launch traced here: 109 us
  starting transfers between devices  37.1 us (34%)
  waiting for transfers between devices  36.6 us (33%)
  blocking collectives  17.2 us (16%)
  Pallas kernels  16.8 us (15%)
    ppermute x14, waiting for transfers between devices, receive(): return lax.ppermute(value, ('dp', 'vocab'), pairs)  28 us
    ppermute x14, starting transfers between devices, receive(): return lax.ppermute(value, ('dp', 'vocab'), pairs)  23.7 us
    all_to_all x1, blocking collectives, shards(): parts = lax.all_to_all(parts, 'dp', 0, 0)  17.2 us
    pallas_call x1, Pallas kernels, update_and_logits(): pl.pallas_call(update_kernel, out_shape=jax.ShapeDtypeStruct(whole, BF16)...  10.2 us
    all_to_all x1, starting transfers between devices, shards(): stat = lax.all_to_all(merge(parts), 'vocab', 0, 0)  9.01 us
    all_to_all x1, waiting for transfers between devices, shards(): stat = lax.all_to_all(merge(parts), 'vocab', 0, 0)  8.69 us
    all_to_all x1, starting transfers between devices, gather(): cot = lax.all_to_all(cot, 'dp', 0, 0)  4.36 us
  transfers between devices with their start and end apart: 16, of which 8 were waited for; matrix products, arithmetic and copies ran while one was open for 0% of the time, Pallas kernels for 3%

profile of v5, /device:TPU:1, one launch (start us, length us, event | category | flops | bytes accessed | tf_op | source)
XLA Modules:
  0.0 109.3 jit_solution(912378754472640596)
XLA Ops:
  0.7 0.1 pad_add_fusion.place
  0.8 2.1 %arrange.1 = (bf16[128,3584]{1,0:T(8,128)(2,1)S(1)}, bf16[128,3584]{1,0:T(8,128)(2,1)S(1)}) custom-call(s32[4]{0:T(128)S(1)} %pad_add_fusion.place, bf16[128,3584]{1,0:T(8,128)(2,1)} %now_ref.3, bf16[128,3584]{1,0:T(8,128)(2,1)} %next_ref.3), custom_call_target="tpu_custom_call" | custom-call | tf_op jit(solution)/shard_map/arrange/pallas_call | solution.py:117
  2.9 2.1 %collective-permute-start = (bf16[128,3584]{1,0:T(8,128)(2,1)S(1)}, bf16[128,3584]{1,0:T(8,128)(2,1)S(1)}, u32[]{:S(2)}, u32[]{:S(2)}) collective-permute-start(bf16[128,3584]{1,0:T(8,128)(2,1)S(1)} %get-tuple-element.11), channel_id=1, source_target_pairs={{32,0},{97,1},{160,128},{225,129},{34,2},{99,3},{162,130},{227,131... | collective-permute-start | bytes 2752520 | tf_op jit(solution)/shard_map/ppermute | solution.py:46
  5.0 5.6 %collective-permute-start.1 = (bf16[128,3584]{1,0:T(8,128)(2,1)S(1)}, bf16[128,3584]{1,0:T(8,128)(2,1)}, u32[]{:S(2)}, u32[]{:S(2)}) collective-permute-start(bf16[128,3584]{1,0:T(8,128)(2,1)S(1)} %get-tuple-element.12), channel_id=1, source_target_pairs={{134,0},{129,1},{0,128},{3,129},{128,2},{131,3},{2,130},{5,131},{1... | collective-permute-start | bytes 2752520 | tf_op jit(solution)/shard_map/ppermute | solution.py:46
  10.6 0.7 copy-done.4
  11.2 1.1 prepare.1
  12.3 5.1 %collective-permute-done.x1_ref.refs_0_ = bf16[128,3584]{1,0:T(8,128)(2,1)S(1)} collective-permute-done((bf16[128,3584]{1,0:T(8,128)(2,1)S(1)}, bf16[128,3584]{1,0:T(8,128)(2,1)S(1)}, u32[]{:S(2)}, u32[]{:S(2)}) %collective-permute-start) | collective-permute-done | bytes 917536 | tf_op jit(solution)/shard_map/ppermute | solution.py:46
  17.4 4.4 %all-to-all-start = ((bf16[8,336,128]{2,1,0:T(8,128)(2,1)}), bf16[8,336,128]{2,1,0:T(8,128)(2,1)S(1)}, u32[]{:S(2)}, u32[]{:S(2)}) async-start(bf16[8,336,128]{2,1,0:T(8,128)(2,1)} %prepare.1), calls=%async_computation | async-start | bytes 1376256 | tf_op jit(solution)/shard_map/all_to_all | solution.py:183
  21.8 5.4 %collective-permute-start.3 = (bf16[128,3584]{1,0:T(8,128)(2,1)S(1)}, bf16[128,3584]{1,0:T(8,128)(2,1)S(1)}, u32[]{:S(2)}, u32[]{:S(2)}) collective-permute-start(bf16[128,3584]{1,0:T(8,128)(2,1)S(1)} %collective-permute-done.x1_ref.refs_0_), channel_id=1, source_target_pairs={{134,0},{129,1},{0,128},{3,129},{128,2},{131,3},{2,130},{5,131},{1... | collective-permute-start | bytes 2752520 | tf_op jit(solution)/shard_map/ppermute | solution.py:46
  27.2 1.3 %collective-permute-start.2 = (bf16[128,3584]{1,0:T(8,128)(2,1)S(1)}, bf16[128,3584]{1,0:T(8,128)(2,1)}, u32[]{:S(2)}, u32[]{:S(2)}) collective-permute-start(bf16[128,3584]{1,0:T(8,128)(2,1)S(1)} %collective-permute-done.x1_ref.refs_0_), channel_id=1, source_target_pairs={{8,0},{25,1},{136,128},{153,129},{10,2},{27,3},{138,130},{155,131}... | collective-permute-start | bytes 2752520 | tf_op jit(solution)/shard_map/ppermute | solution.py:46
  28.5 1.0 rearranged.2
  29.5 1.3 %collective-permute-start.4 = (bf16[128,3584]{1,0:T(8,128)(2,1)S(1)}, bf16[128,3584]{1,0:T(8,128)(2,1)S(1)}, u32[]{:S(2)}, u32[]{:S(2)}) collective-permute-start(bf16[128,3584]{1,0:T(8,128)(2,1)S(1)} %rearranged.2), channel_id=1, source_target_pairs={{32,0},{97,1},{160,128},{225,129},{34,2},{99,3},{162,130},{227,131... | collective-permute-start | bytes 2752520 | tf_op jit(solution)/shard_map/ppermute | solution.py:46
  30.8 2.5 %collective-permute-start.7 = (bf16[128,3584]{1,0:T(8,128)(2,1)S(1)}, bf16[128,3584]{1,0:T(8,128)(2,1)}, u32[]{:S(2)}, u32[]{:S(2)}) collective-permute-start(bf16[128,3584]{1,0:T(8,128)(2,1)S(1)} %collective-permute-done.x1_ref.refs_0_), channel_id=1, source_target_pairs={{1,0},{0,1},{129,128},{128,129},{3,2},{2,3},{131,130},{130,131},{5... | collective-permute-start | bytes 2752520 | tf_op jit(solution)/shard_map/ppermute | solution.py:46
  33.3 8.6 %collective-permute-done.3.z2_ref.refs_3_ = bf16[128,3584]{1,0:T(8,128)(2,1)S(1)} collective-permute-done((bf16[128,3584]{1,0:T(8,128)(2,1)S(1)}, bf16[128,3584]{1,0:T(8,128)(2,1)S(1)}, u32[]{:S(2)}, u32[]{:S(2)}) %collective-permute-start.3) | collective-permute-done | bytes 917536 | tf_op jit(solution)/shard_map/ppermute | solution.py:46
  41.9 2.3 %collective-permute-done.4.x2_ref.refs_4_ = bf16[128,3584]{1,0:T(8,128)(2,1)S(1)} collective-permute-done((bf16[128,3584]{1,0:T(8,128)(2,1)S(1)}, bf16[128,3584]{1,0:T(8,128)(2,1)S(1)}, u32[]{:S(2)}, u32[]{:S(2)}) %collective-permute-start.4) | collective-permute-done | bytes 917536 | tf_op jit(solution)/shard_map/ppermute | solution.py:46
  44.2 0.1 rearranged.3
  44.4 1.4 %collective-permute-start.5 = (bf16[128,3584]{1,0:T(8,128)(2,1)S(1)}, bf16[128,3584]{1,0:T(8,128)(2,1)S(1)}, u32[]{:S(2)}, u32[]{:S(2)}) collective-permute-start(bf16[128,3584]{1,0:T(8,128)(2,1)S(1)} %get-tuple-element.17), channel_id=1, source_target_pairs={{8,0},{25,1},{136,128},{153,129},{10,2},{27,3},{138,130},{155,131}... | collective-permute-start | bytes 2752520 | tf_op jit(solution)/shard_map/ppermute | solution.py:46
  45.7 3.1 %collective-permute-start.10 = (bf16[128,3584]{1,0:T(8,128)(2,1)S(1)}, bf16[128,3584]{1,0:T(8,128)(2,1)S(1)}, u32[]{:S(2)}, u32[]{:S(2)}) collective-permute-start(bf16[128,3584]{1,0:T(8,128)(2,1)S(1)} %collective-permute-done.3.z2_ref.refs_3_), channel_id=1, source_target_pairs={{1,0},{0,1},{129,128},{128,129},{3,2},{2,3},{131,130},{130,131},{5... | collective-permute-start | bytes 2752520 | tf_op jit(solution)/shard_map/ppermute | solution.py:46
  48.8 0.0 collective-permute-start.11
  48.9 0.5 collective-permute-start.9
  49.4 8.5 %collective-permute-done.5.refs_5_ = bf16[128,3584]{1,0:T(8,128)(2,1)S(1)} collective-permute-done((bf16[128,3584]{1,0:T(8,128)(2,1)S(1)}, bf16[128,3584]{1,0:T(8,128)(2,1)S(1)}, u32[]{:S(2)}, u32[]{:S(2)}) %collective-permute-start.5) | collective-permute-done | bytes 917536 | tf_op jit(solution)/shard_map/ppermute | solution.py:46
  57.9 1.3 %collective-permute-done.6.refs_6_ = bf16[128,3584]{1,0:T(8,128)(2,1)S(1)} collective-permute-done((bf16[128,3584]{1,0:T(8,128)(2,1)S(1)}, bf16[128,3584]{1,0:T(8,128)(2,1)S(1)}, u32[]{:S(2)}, u32[]{:S(2)}) %collective-permute-start.6) | collective-permute-done | bytes 917536 | tf_op jit(solution)/shard_map/ppermute | solution.py:46
  59.2 0.6 collective-permute-start.13
  59.8 0.6 collective-permute-done.12.refs_12_
  60.4 1.5 %collective-permute-done.13.refs_13_ = bf16[128,3584]{1,0:T(8,128)(2,1)S(1)} collective-permute-done((bf16[128,3584]{1,0:T(8,128)(2,1)S(1)}, bf16[128,3584]{1,0:T(8,128)(2,1)S(1)}, u32[]{:S(2)}, u32[]{:S(2)}) %collective-permute-start.13) | collective-permute-done | bytes 917536 | tf_op jit(solution)/shard_map/ppermute | solution.py:46
  61.9 10.2 %update_and_logits.1 = bf16[8,336,128]{2,1,0:T(8,128)(2,1)S(1)} custom-call(s32[4]{0:T(128)S(1)} %pad_add_fusion.place, bf16[128,3584]{1,0:T(8,128)(2,1)} %now_ref.3, bf16[128,3584]{1,0:T(8,128)(2,1)} %next_ref.3, bf16[128,3584]{1,0:T(8,128)(2,1)} %copy-done.2, bf16[128,3584]{1,0:T(8,128)(2,1)} %collective-permute-done.1.z1_ref.refs_1_, ...), custom_call_target="tpu_custom_call" | custom-call | flops 9400000512 | bytes 24000000 | tf_op jit(solution)/shard_map/update_and_logits/pallas_call | solution.py:274
  72.0 17.2 %all_to_all.15.part_ref = bf16[8,336,128]{2,1,0:T(8,128)(2,1)S(1)} all-to-all(bf16[8,336,128]{2,1,0:T(8,128)(2,1)S(1)} %update_and_logits.1), channel_id=1, replica_groups=mesh['dp'=8,'vocab'=32] {'dp'}, dimensions={0} | all-to-all | bytes 1376256 | tf_op jit(solution)/shard_map/all_to_all | solution.py:360
  89.2 0.7 merge.1
  89.9 9.0 %all-to-all-start.2 = ((f32[32,3,128]{2,1,0:T(4,128)}), f32[32,3,128]{2,1,0:T(4,128)S(1)}, u32[]{:S(2)}, u32[]{:S(2)}) async-start(f32[32,3,128]{2,1,0:T(4,128)} %merge.1), calls=%async_computation.2 | async-start | bytes 131072 | tf_op jit(solution)/shard_map/all_to_all | solution.py:361
  98.9 1.1 turn.1
  100.0 8.7 %all-to-all-done.2.stat_ref = f32[32,3,128]{2,1,0:T(4,128)S(1)} async-done(((f32[32,3,128]{2,1,0:T(4,128)}), f32[32,3,128]{2,1,0:T(4,128)S(1)}, u32[]{:S(2)}, u32[]{:S(2)}) %all-to-all-start.2) | async-done | bytes 49184 | tf_op jit(solution)/shard_map/all_to_all | solution.py:361
  108.7 0.6 loss.1
  (26 shorter events, 0.1 us)
Async XLA Ops:
  0.6 9.9 %copy-start.3 = (bf16[128,2560]{1,0:T(8,128)(2,1)S(1)}, bf16[128,2560]{1,0:T(8,128)(2,1)}, u32[]{:S(2)}) copy-start(bf16[128,2560]{1,0:T(8,128)(2,1)} %cot_ref.1) | copy-start | bytes 1966084
  2.9 14.6 %collective-permute-start = (bf16[128,3584]{1,0:T(8,128)(2,1)S(1)}, bf16[128,3584]{1,0:T(8,128)(2,1)S(1)}, u32[]{:S(2)}, u32[]{:S(2)}) collective-permute-start(bf16[128,3584]{1,0:T(8,128)(2,1)S(1)} %get-tuple-element.11), channel_id=1, source_target_pairs={{32,0},{97,1},{160,128},{225,129},{34,2},{99,3},{162,130},{227,131... | collective-permute-start | bytes 2752520 | tf_op jit(solution)/shard_map/ppermute | solution.py:46
  5.0 23.5 %collective-permute-start.1 = (bf16[128,3584]{1,0:T(8,128)(2,1)S(1)}, bf16[128,3584]{1,0:T(8,128)(2,1)}, u32[]{:S(2)}, u32[]{:S(2)}) collective-permute-start(bf16[128,3584]{1,0:T(8,128)(2,1)S(1)} %get-tuple-element.12), channel_id=1, source_target_pairs={{134,0},{129,1},{0,128},{3,129},{128,2},{131,3},{2,130},{5,131},{1... | collective-permute-start | bytes 2752520 | tf_op jit(solution)/shard_map/ppermute | solution.py:46
  10.6 0.7 copy-start.4
  17.4 26.9 %copy-start.2 = (bf16[128,3584]{1,0:T(8,128)(2,1)}, bf16[128,3584]{1,0:T(8,128)(2,1)S(1)}, u32[]{:S(2)}) copy-start(bf16[128,3584]{1,0:T(8,128)(2,1)S(1)} %collective-permute-done.x1_ref.refs_0_) | copy-start | bytes 2752516
  17.4 26.8 %all-to-all-start = ((bf16[8,336,128]{2,1,0:T(8,128)(2,1)}), bf16[8,336,128]{2,1,0:T(8,128)(2,1)S(1)}, u32[]{:S(2)}, u32[]{:S(2)}) async-start(bf16[8,336,128]{2,1,0:T(8,128)(2,1)} %prepare.1), calls=%async_computation | async-start | bytes 1376256 | tf_op jit(solution)/shard_map/all_to_all | solution.py:183
  21.8 20.1 %collective-permute-start.3 = (bf16[128,3584]{1,0:T(8,128)(2,1)S(1)}, bf16[128,3584]{1,0:T(8,128)(2,1)S(1)}, u32[]{:S(2)}, u32[]{:S(2)}) collective-permute-start(bf16[128,3584]{1,0:T(8,128)(2,1)S(1)} %collective-permute-done.x1_ref.refs_0_), channel_id=1, source_target_pairs={{134,0},{129,1},{0,128},{3,129},{128,2},{131,3},{2,130},{5,131},{1... | collective-permute-start | bytes 2752520 | tf_op jit(solution)/shard_map/ppermute | solution.py:46
  27.2 14.7 %collective-permute-start.2 = (bf16[128,3584]{1,0:T(8,128)(2,1)S(1)}, bf16[128,3584]{1,0:T(8,128)(2,1)}, u32[]{:S(2)}, u32[]{:S(2)}) collective-permute-start(bf16[128,3584]{1,0:T(8,128)(2,1)S(1)} %collective-permute-done.x1_ref.refs_0_), channel_id=1, source_target_pairs={{8,0},{25,1},{136,128},{153,129},{10,2},{27,3},{138,130},{155,131}... | collective-permute-start | bytes 2752520 | tf_op jit(solution)/shard_map/ppermute | solution.py:46
  29.5 14.7 %collective-permute-start.4 = (bf16[128,3584]{1,0:T(8,128)(2,1)S(1)}, bf16[128,3584]{1,0:T(8,128)(2,1)S(1)}, u32[]{:S(2)}, u32[]{:S(2)}) collective-permute-start(bf16[128,3584]{1,0:T(8,128)(2,1)S(1)} %rearranged.2), channel_id=1, source_target_pairs={{32,0},{97,1},{160,128},{225,129},{34,2},{99,3},{162,130},{227,131... | collective-permute-start | bytes 2752520 | tf_op jit(solution)/shard_map/ppermute | solution.py:46
  30.8 18.0 %collective-permute-start.7 = (bf16[128,3584]{1,0:T(8,128)(2,1)S(1)}, bf16[128,3584]{1,0:T(8,128)(2,1)}, u32[]{:S(2)}, u32[]{:S(2)}) collective-permute-start(bf16[128,3584]{1,0:T(8,128)(2,1)S(1)} %collective-permute-done.x1_ref.refs_0_), channel_id=1, source_target_pairs={{1,0},{0,1},{129,128},{128,129},{3,2},{2,3},{131,130},{130,131},{5... | collective-permute-start | bytes 2752520 | tf_op jit(solution)/shard_map/ppermute | solution.py:46
  33.3 15.6 %collective-permute-start.8 = (bf16[128,3584]{1,0:T(8,128)(2,1)}, bf16[128,3584]{1,0:T(8,128)(2,1)}, u32[]{:S(2)}, u32[]{:S(2)}) collective-permute-start(bf16[128,3584]{1,0:T(8,128)(2,1)} %collective-permute-done.1.z1_ref.refs_1_), channel_id=1, source_target_pairs={{1,0},{0,1},{129,128},{128,129},{3,2},{2,3},{131,130},{130,131},{5... | collective-permute-start | bytes 2752520 | tf_op jit(solution)/shard_map/ppermute | solution.py:46
  41.9 19.9 %copy-start = (bf16[128,3584]{1,0:T(8,128)(2,1)}, bf16[128,3584]{1,0:T(8,128)(2,1)S(1)}, u32[]{:S(2)}) copy-start(bf16[128,3584]{1,0:T(8,128)(2,1)S(1)} %collective-permute-done.3.z2_ref.refs_3_) | copy-start | bytes 2752516
  44.2 17.6 %copy-start.1 = (bf16[128,3584]{1,0:T(8,128)(2,1)}, bf16[128,3584]{1,0:T(8,128)(2,1)S(1)}, u32[]{:S(2)}) copy-start(bf16[128,3584]{1,0:T(8,128)(2,1)S(1)} %collective-permute-done.4.x2_ref.refs_4_) | copy-start | bytes 2752516
  44.4 13.5 %collective-permute-start.5 = (bf16[128,3584]{1,0:T(8,128)(2,1)S(1)}, bf16[128,3584]{1,0:T(8,128)(2,1)S(1)}, u32[]{:S(2)}, u32[]{:S(2)}) collective-permute-start(bf16[128,3584]{1,0:T(8,128)(2,1)S(1)} %get-tuple-element.17), channel_id=1, source_target_pairs={{8,0},{25,1},{136,128},{153,129},{10,2},{27,3},{138,130},{155,131}... | collective-permute-start | bytes 2752520 | tf_op jit(solution)/shard_map/ppermute | solution.py:46
  45.7 13.5 %collective-permute-start.6 = (bf16[128,3584]{1,0:T(8,128)(2,1)S(1)}, bf16[128,3584]{1,0:T(8,128)(2,1)S(1)}, u32[]{:S(2)}, u32[]{:S(2)}) collective-permute-start(bf16[128,3584]{1,0:T(8,128)(2,1)S(1)} %get-tuple-element.18), channel_id=1, source_target_pairs={{32,0},{97,1},{160,128},{225,129},{34,2},{99,3},{162,130},{227,131... | collective-permute-start | bytes 2752520 | tf_op jit(solution)/shard_map/ppermute | solution.py:46
  45.7 14.0 %collective-permute-start.10 = (bf16[128,3584]{1,0:T(8,128)(2,1)S(1)}, bf16[128,3584]{1,0:T(8,128)(2,1)S(1)}, u32[]{:S(2)}, u32[]{:S(2)}) collective-permute-start(bf16[128,3584]{1,0:T(8,128)(2,1)S(1)} %collective-permute-done.3.z2_ref.refs_3_), channel_id=1, source_target_pairs={{1,0},{0,1},{129,128},{128,129},{3,2},{2,3},{131,130},{130,131},{5... | collective-permute-start | bytes 2752520 | tf_op jit(solution)/shard_map/ppermute | solution.py:46
  48.8 10.9 %collective-permute-start.11 = (bf16[128,3584]{1,0:T(8,128)(2,1)S(1)}, bf16[128,3584]{1,0:T(8,128)(2,1)S(1)}, u32[]{:S(2)}, u32[]{:S(2)}) collective-permute-start(bf16[128,3584]{1,0:T(8,128)(2,1)S(1)} %collective-permute-done.4.x2_ref.refs_4_), channel_id=1, source_target_pairs={{1,0},{0,1},{129,128},{128,129},{3,2},{2,3},{131,130},{130,131},{5... | collective-permute-start | bytes 2752520 | tf_op jit(solution)/shard_map/ppermute | solution.py:46
  48.9 10.9 %collective-permute-start.9 = (bf16[128,3584]{1,0:T(8,128)(2,1)}, bf16[128,3584]{1,0:T(8,128)(2,1)S(1)}, u32[]{:S(2)}, u32[]{:S(2)}) collective-permute-start(bf16[128,3584]{1,0:T(8,128)(2,1)} %collective-permute-done.2.refs_2_), channel_id=1, source_target_pairs={{1,0},{0,1},{129,128},{128,129},{3,2},{2,3},{131,130},{130,131},{5... | collective-permute-start | bytes 2752520 | tf_op jit(solution)/shard_map/ppermute | solution.py:46
  57.9 2.5 %collective-permute-start.12 = (bf16[128,3584]{1,0:T(8,128)(2,1)S(1)}, bf16[128,3584]{1,0:T(8,128)(2,1)S(1)}, u32[]{:S(2)}, u32[]{:S(2)}) collective-permute-start(bf16[128,3584]{1,0:T(8,128)(2,1)S(1)} %collective-permute-done.5.refs_5_), channel_id=1, source_target_pairs={{1,0},{0,1},{129,128},{128,129},{3,2},{2,3},{131,130},{130,131},{5... | collective-permute-start | bytes 2752520 | tf_op jit(solution)/shard_map/ppermute | solution.py:46
  59.2 2.7 %collective-permute-start.13 = (bf16[128,3584]{1,0:T(8,128)(2,1)S(1)}, bf16[128,3584]{1,0:T(8,128)(2,1)S(1)}, u32[]{:S(2)}, u32[]{:S(2)}) collective-permute-start(bf16[128,3584]{1,0:T(8,128)(2,1)S(1)} %collective-permute-done.6.refs_6_), channel_id=1, source_target_pairs={{1,0},{0,1},{129,128},{128,129},{3,2},{2,3},{131,130},{130,131},{5... | collective-permute-start | bytes 2752520 | tf_op jit(solution)/shard_map/ppermute | solution.py:46
  59.8 2.1 %copy-start.7 = (bf16[128,3584]{1,0:T(8,128)(2,1)}, bf16[128,3584]{1,0:T(8,128)(2,1)S(1)}, u32[]{:S(2)}) copy-start(bf16[128,3584]{1,0:T(8,128)(2,1)S(1)} %collective-permute-done.9.refs_9_) | copy-start | bytes 2752516
  59.8 2.1 %copy-start.5 = (bf16[128,3584]{1,0:T(8,128)(2,1)}, bf16[128,3584]{1,0:T(8,128)(2,1)S(1)}, u32[]{:S(2)}) copy-start(bf16[128,3584]{1,0:T(8,128)(2,1)S(1)} %collective-permute-done.10.refs_10_) | copy-start | bytes 2752516
  59.8 2.1 %copy-start.6 = (bf16[128,3584]{1,0:T(8,128)(2,1)}, bf16[128,3584]{1,0:T(8,128)(2,1)S(1)}, u32[]{:S(2)}) copy-start(bf16[128,3584]{1,0:T(8,128)(2,1)S(1)} %collective-permute-done.11.refs_11_) | copy-start | bytes 2752516
  89.9 18.8 %all-to-all-start.2 = ((f32[32,3,128]{2,1,0:T(4,128)}), f32[32,3,128]{2,1,0:T(4,128)S(1)}, u32[]{:S(2)}, u32[]{:S(2)}) async-start(f32[32,3,128]{2,1,0:T(4,128)} %merge.1), calls=%async_computation.2 | async-start | bytes 131072 | tf_op jit(solution)/shard_map/all_to_all | solution.py:361
